TPU v7x, 32 devices: a whole 2x2x4 slice. The times are simulated.
32 devices in a mesh: row: 4 (over z), col: 8 (over y, x, core).
Axes of the slice: x: 2, y: 2, z: 4, core: 2. Of those that a mesh axis runs over, the one named last changes fastest.
Arguments:
- ancestor: float32 [16384, 16384], P('row', 'col'), may hold values from -6 to 6
- factor: float32 [2, 16384, 512], P(None, ('row', 'col')), may hold values from -0.0625 to 0.0625
- diag_inverse: float32 [2, 512, 512], replicated, may hold values from -6 to 6
- structure: int32 [2, 16], replicated, may hold values from 0 to 31, as said below
Outputs:
- off_diagonal: float32 [2, 16384, 512], P(None, ('row', 'col'))
- diag_block: float32 [2, 512, 512], replicated
Inputs may be any that keep to these rules, and one draw needn't show every extreme that they name: `structure`: each row holds 16 distinct tile indices; tile t covers rows t * 512 to t * 512 + 511.
All inputs are finite; a program needn't handle non-finite values.
Results may differ from a plain program's by a relative error of at most 0.0001.
Values sent between devices are 32-bit elements; how exact they have to be, the bound alone decides.
A program may use at most 128 MiB of HBM per device.

v0:
```python
import jax
import jax.numpy as jnp
from jax import lax
from jax.sharding import PartitionSpec as P

TILE = 512
WIDTH = 512


exact_mode = lax.Precision.HIGHEST


def from_root(block, axis, holder):
    block = jnp.where(lax.axis_index(axis) == holder, block, jnp.zeros_like(block))
    return lax.psum(block, axis)


def tile_table(structure, tile_ids):
    hits = structure[:, :, None] == tile_ids[None, None, :]
    return jnp.any(hits, axis=1).astype(jnp.float32)


def panel_product(ancestor, right_cols, tile_flags):
    tile_count = tile_flags.shape[0]
    blocks = ancestor.reshape(tile_count, TILE, ancestor.shape[1])

    def one_tile(operands):
        tile_block, flag_value = operands
        return lax.cond(
            flag_value > 0.0,
            lambda tile_rows: jnp.dot(
                tile_rows, right_cols, precision=exact_mode, preferred_element_type=jnp.float32
            ),
            lambda tile_rows: jnp.zeros((tile_rows.shape[0], right_cols.shape[1]), jnp.float32),
            tile_block,
        )

    stacked = lax.map(one_tile, (blocks, tile_flags))
    return stacked.reshape(ancestor.shape[0], right_cols.shape[1])


def per_device(ancestor, factor, diag_inverse, structure):
    row_index = lax.axis_index("row")
    col_index = lax.axis_index("col")
    rows_local = ancestor.shape[0]
    cols_local = ancestor.shape[1]
    shard_rows = factor.shape[1]
    ratio_cols = lax.axis_size("col") // lax.axis_size("row")
    row_tiles = row_index * (rows_local // TILE) + jnp.arange(rows_local // TILE, dtype=jnp.int32)
    col_tiles = col_index * (cols_local // TILE) + jnp.arange(cols_local // TILE, dtype=jnp.int32)
    row_table = tile_table(structure, row_tiles)
    col_table = tile_table(structure, col_tiles)
    row_mask = jnp.repeat(row_table, TILE, axis=1)
    col_mask = jnp.repeat(col_table, TILE, axis=1)
    start_row = (row_index * lax.axis_size("col") + col_index) * shard_rows
    own_tiles = (start_row + jnp.arange(shard_rows, dtype=jnp.int32)) // TILE
    own_mask = tile_table(structure, own_tiles)
    offset_rows = col_index % ratio_cols * cols_local
    root_row = col_index // ratio_cols
    grouped = lax.all_gather(factor, "col", axis=1, tiled=True)
    own_half = lax.dynamic_slice_in_dim(grouped, offset_rows, cols_local, 1)
    column_block = from_root(own_half, "row", root_row)
    masked = column_block * col_mask[:, :, None]
    right_cols = jnp.concatenate([masked[0], masked[1]], axis=1)
    tile_flags = jnp.max(row_table, axis=0) * jnp.max(col_table)
    product = panel_product(ancestor, right_cols, tile_flags)
    partial_value = jnp.stack([product[:, :WIDTH], product[:, WIDTH:]]) * row_mask[:, :, None]
    panel_rows = lax.psum_scatter(partial_value, "col", scatter_dimension=1, tiled=True)
    own_factor = factor * own_mask[:, :, None]
    diag_terms = jnp.einsum("kri,krj->kij", own_factor, panel_rows, precision=exact_mode)
    summed = lax.psum(diag_terms, ("row", "col"))
    return (-panel_rows, diag_inverse + summed)


def solution(mesh):
    in_specs = (P("row", "col"), P(None, ("row", "col"), None), P(), P())
    out_specs = (P(None, ("row", "col"), None), P())
    return jax.shard_map(
        per_device, mesh=mesh, in_specs=in_specs, out_specs=out_specs, check_vma=False
    )
```

profile of v0, /device:TPU:1, one launch (start us, length us, event | category | flops | bytes accessed | tf_op | source)
XLA Modules:
  0.0 826.5 jit_solution(7149627261888457539)
XLA Ops:
  7.2 0.7 all-gather.2.cloned.1.call-update
  8.0 94.3 %all-gather.2.cloned.1.call-done = f32[2,4096,512]{2,1,0:T(8,128)} async-done(((f32[2,512,512]{2,1,0:T(8,128)}), f32[2,4096,512]{2,1,0:T(8,128)}) %all-gather.2.cloned.1.call-update) | async-done | bytes 16777232 | tf_op jit(solution)/shard_map/all_gather | solution.py:60
  102.3 7.6 dynamic-slice_select_fusion
  110.0 0.6 copy-done.1
  111.2 0.6 convert_reduce_fusion
  111.8 0.6 broadcast_multiply_fusion.1
  112.5 288.0 %all-reduce.3.cloned.1.call-done = f32[2,2048,512]{2,1,0:T(8,128)} async-done(((f32[2,2048,512]{2,1,0:T(8,128)}), f32[2,2048,512]{2,1,0:T(8,128)}) %all-reduce.3.cloned.1.call-update) | async-done | bytes 8388624 | tf_op jit(solution)/shard_map/psum | solution.py:15
  400.5 3.8 broadcast_multiply_fusion
  404.4 1.0 slice_bitcast_fusion.3
  405.3 4.2 pad_maximum_fusion
  409.5 105.9 %while.10 = (s32[]{:T(128)}, f32[8,512,1024]{2,1,0:T(8,128)}, f32[8]{0:T(128)S(1)}, f32[8,512,2048]{2,1,0:T(8,128)}, f32[2048,1024]{1,0:T(8,128)}, /*index=5*/s32[]{:T(128)}, f32[1]{0:T(128)}) while((s32[]{:T(128)}, f32[8,512,1024]{2,1,0:T(8,128)}, f32[8]{0:T(128)S(1)}, f32[8,512,2048]{2,1,0:T(8,128)}, f32[2048,1024]{1,0:T(8,128)}, ...), condition=%wide.region_8.9_spmd, body=%wide.region_5.8_spmd.sunk | while | flops 12884901888 | bytes 18875528 | solution.py:38
  409.5 0.6 dynamic_slice.23
  410.8 16.7 %conditional.2 = (f32[1,512,1024]{2,1,0:T(8,128)S(1)}) conditional(s32[]{:T(128)} %bitcast.27, () %tuple.36, (f32[8,512,2048]{2,1,0:T(8,128)}, s32[]{:T(128)}, f32[2048,1024]{1,0:T(8,128)}) %tuple.37), branch_computations={%region_6.6_spmd, %region_7.7_spmd} | conditional | flops 12884901888 | bytes 14680584 | solution.py:29
  410.8 16.7 %fusion.3 = f32[1,512,1024]{2,1,0:T(8,128)S(1)} fusion(f32[2048,1024]{1,0:T(8,128)} %get-tuple-element.41, f32[8,512,2048]{2,1,0:T(8,128)} %get-tuple-element.39, s32[]{:T(128)} %get-tuple-element.40), kind=kOutput, calls=%fused_computation.3 | convolution fusion | flops 12884901888 | bytes 14680576 | tf_op jit(solution)/shard_map/while/body/eval_jaxpr/cond/branch_1_fun/dot_general | solution.py:31
  427.4 1.5 constant_dynamic-update-slice_fusion.2
  428.9 0.6 dynamic_slice.23
  430.2 16.7 %conditional.2 = (f32[1,512,1024]{2,1,0:T(8,128)S(1)}) conditional(s32[]{:T(128)} %bitcast.27, () %tuple.36, (f32[8,512,2048]{2,1,0:T(8,128)}, s32[]{:T(128)}, f32[2048,1024]{1,0:T(8,128)}) %tuple.37), branch_computations={%region_6.6_spmd, %region_7.7_spmd} | conditional | flops 12884901888 | bytes 14680584 | solution.py:29
  430.2 16.7 %fusion.3 = f32[1,512,1024]{2,1,0:T(8,128)S(1)} fusion(f32[2048,1024]{1,0:T(8,128)} %get-tuple-element.41, f32[8,512,2048]{2,1,0:T(8,128)} %get-tuple-element.39, s32[]{:T(128)} %get-tuple-element.40), kind=kOutput, calls=%fused_computation.3 | convolution fusion | flops 12884901888 | bytes 14680576 | tf_op jit(solution)/shard_map/while/body/eval_jaxpr/cond/branch_1_fun/dot_general | solution.py:31
  446.9 1.4 constant_dynamic-update-slice_fusion.2
  448.3 0.6 dynamic_slice.23
  449.5 0.3 conditional.2
  449.5 0.2 broadcast_in_dim.7
  449.8 1.5 constant_dynamic-update-slice_fusion.2
  451.3 0.6 dynamic_slice.23
  452.5 16.7 %conditional.2 = (f32[1,512,1024]{2,1,0:T(8,128)S(1)}) conditional(s32[]{:T(128)} %bitcast.27, () %tuple.36, (f32[8,512,2048]{2,1,0:T(8,128)}, s32[]{:T(128)}, f32[2048,1024]{1,0:T(8,128)}) %tuple.37), branch_computations={%region_6.6_spmd, %region_7.7_spmd} | conditional | flops 12884901888 | bytes 14680584 | solution.py:29
  452.5 16.7 %fusion.3 = f32[1,512,1024]{2,1,0:T(8,128)S(1)} fusion(f32[2048,1024]{1,0:T(8,128)} %get-tuple-element.41, f32[8,512,2048]{2,1,0:T(8,128)} %get-tuple-element.39, s32[]{:T(128)} %get-tuple-element.40), kind=kOutput, calls=%fused_computation.3 | convolution fusion | flops 12884901888 | bytes 14680576 | tf_op jit(solution)/shard_map/while/body/eval_jaxpr/cond/branch_1_fun/dot_general | solution.py:31
  469.2 1.5 constant_dynamic-update-slice_fusion.2
  470.7 0.6 dynamic_slice.23
  471.9 16.7 %conditional.2 = (f32[1,512,1024]{2,1,0:T(8,128)S(1)}) conditional(s32[]{:T(128)} %bitcast.27, () %tuple.36, (f32[8,512,2048]{2,1,0:T(8,128)}, s32[]{:T(128)}, f32[2048,1024]{1,0:T(8,128)}) %tuple.37), branch_computations={%region_6.6_spmd, %region_7.7_spmd} | conditional | flops 12884901888 | bytes 14680584 | solution.py:29
  471.9 16.7 %fusion.3 = f32[1,512,1024]{2,1,0:T(8,128)S(1)} fusion(f32[2048,1024]{1,0:T(8,128)} %get-tuple-element.41, f32[8,512,2048]{2,1,0:T(8,128)} %get-tuple-element.39, s32[]{:T(128)} %get-tuple-element.40), kind=kOutput, calls=%fused_computation.3 | convolution fusion | flops 12884901888 | bytes 14680576 | tf_op jit(solution)/shard_map/while/body/eval_jaxpr/cond/branch_1_fun/dot_general | solution.py:31
  488.6 1.5 constant_dynamic-update-slice_fusion.2
  490.1 0.6 dynamic_slice.23
  491.4 0.3 conditional.2
  491.6 1.4 constant_dynamic-update-slice_fusion.2
  493.1 0.6 dynamic_slice.23
  494.3 16.7 %conditional.2 = (f32[1,512,1024]{2,1,0:T(8,128)S(1)}) conditional(s32[]{:T(128)} %bitcast.27, () %tuple.36, (f32[8,512,2048]{2,1,0:T(8,128)}, s32[]{:T(128)}, f32[2048,1024]{1,0:T(8,128)}) %tuple.37), branch_computations={%region_6.6_spmd, %region_7.7_spmd} | conditional | flops 12884901888 | bytes 14680584 | solution.py:29
  494.3 16.7 %fusion.3 = f32[1,512,1024]{2,1,0:T(8,128)S(1)} fusion(f32[2048,1024]{1,0:T(8,128)} %get-tuple-element.41, f32[8,512,2048]{2,1,0:T(8,128)} %get-tuple-element.39, s32[]{:T(128)} %get-tuple-element.40), kind=kOutput, calls=%fused_computation.3 | convolution fusion | flops 12884901888 | bytes 14680576 | tf_op jit(solution)/shard_map/while/body/eval_jaxpr/cond/branch_1_fun/dot_general | solution.py:31
  511.0 1.5 constant_dynamic-update-slice_fusion.2
  512.5 0.6 dynamic_slice.23
  513.7 0.3 conditional.2
  514.0 1.5 constant_dynamic-update-slice_fusion.2
  515.5 6.9 slice_bitcast_fusion.1
  522.3 6.1 maximum_multiply_fusion
  528.8 147.6 %reduce-scatter.2.cloned.1.call-done = f32[2,512,512]{2,1,0:T(8,128)} async-done(((f32[2,4096,512]{2,1,0:T(8,128)}), f32[2,512,512]{2,1,0:T(8,128)}) %reduce-scatter.2.cloned.1.call-update) | async-done | bytes 2097168 | tf_op jit(solution)/shard_map/reduce_scatter | solution.py:68
  676.4 6.7 fusion.7
  683.1 3.1 neg.3
  686.2 129.8 %all-reduce.5.cloned.1.call-done = f32[2,512,512]{2,1,0:T(8,128)} async-done(((f32[2,512,512]{2,1,0:T(8,128)}), f32[2,512,512]{2,1,0:T(8,128)}) %all-reduce.5.cloned.1.call-update) | async-done | bytes 2097168 | tf_op jit(solution)/shard_map/psum | solution.py:71
  816.0 4.0 add.67
  (27 shorter events, 1.6 us)
Async XLA Ops:
  7.2 95.1 %all-gather.2.cloned.1.call-start = ((), (), s32[]{:S(2)}) async-start(), calls=%async_computation.1 | async-start | bytes 18874368 | tf_op jit(solution)/shard_map/all_gather | solution.py:60
  7.9 392.6 %all-reduce.3.cloned.1.call-start = ((), (), s32[]{:S(2)}) async-start(), calls=%async_computation.2 | async-start | bytes 16777216 | tf_op jit(solution)/shard_map/psum | solution.py:15
  109.9 0.7 copy-start.1
  110.0 566.4 %reduce-scatter.2.cloned.1.call-start = ((), (), s32[]{:S(2)}) async-start(), calls=%async_computation.3 | async-start | bytes 18874368 | tf_op jit(solution)/shard_map/reduce_scatter | solution.py:68
  528.4 148.0 %copy-start = (f32[2,512,512]{2,1,0:T(8,128)S(1)}, f32[2,512,512]{2,1,0:T(8,128)}, u32[]{:S(2)}) copy-start(f32[2,512,512]{2,1,0:T(8,128)} %param.9) | copy-start | bytes 6291460
  528.4 287.6 %all-reduce.5.cloned.1.call-start = ((), (), s32[]{:S(2)}) async-start(), calls=%async_computation.4 | async-start | bytes 4194304 | tf_op jit(solution)/shard_map/psum | solution.py:71
Sparse Core Ops, SparseCore 0:
  9.9 92.3 all-gather.1
  110.1 290.3 all-reduce.2
  528.5 147.7 reduce-scatter.1
  683.2 132.7 all-reduce.4
where the time goes:
time: 829 us; the launch traced here: 827 us
  waiting for transfers between devices  660 us (80%)
  matrix products  90 us (11%)
  other arithmetic  30.6 us (4%)
  local copies, waits for them, and re-layouts  25.8 us (3%)
  between operations  13.9 us (2%)
    psum x1, waiting for transfers between devices, from_root(): return lax.psum(block, axis)  288 us
    reduce_scatter x1, waiting for transfers between devices, per_device(): lax.psum_scatter(partial_value, 'col', scatter_dimension=1, tiled=True)  148 us
    psum x1, waiting for transfers between devices, per_device(): summed = lax.psum(diag_terms, ('row', 'col'))  130 us
    all_gather x1, waiting for transfers between devices, per_device(): grouped = lax.all_gather(factor, 'col', axis=1, tiled=True)  94.3 us
    dot_general x5, matrix products, one_tile(): jnp.dot(tile_rows, right_cols, precision=exact_mode, preferred_element_ty...  83.3 us
  transfers between devices with their start and end apart: 4, of which 4 were waited for; matrix products, arithmetic and copies ran while one was open for 1% of the time, Pallas kernels for 0%

commit v1 on v0

v1 whole, which is shorter than its diff:
```python
import functools

import jax
import jax.numpy as jnp
from jax import lax
from jax.experimental import pallas as pl
from jax.experimental.pallas import tpu as pltpu
from jax.sharding import PartitionSpec as P

TILE = 512


def tile_table(structure, tile_ids):
    hits = structure[:, :, None] == tile_ids[None, None, :]
    return jnp.any(hits, axis=1).astype(jnp.int32)


def product_kernel(rows, pieces, meta, a_ref, *refs):
    f_refs, out_ref, high, low = refs[:pieces], refs[pieces], refs[-2], refs[-1]
    step = pl.program_id(0)
    depth = high.shape[1]

    @pl.when(step == 0)
    def _():
        for q in range(pieces):
            whole = f_refs[q][...]
            top = whole.astype(jnp.bfloat16)
            high[q] = top
            low[q] = (whole - top.astype(jnp.float32)).astype(jnp.bfloat16)

    out_ref[...] = jnp.zeros_like(out_ref)

    @pl.when(meta[rows + step] > 0)
    def _():
        @pl.loop(0, pieces)
        def _(q):
            @pl.when(meta[2 * rows + q] > 0)
            def _():
                start = pl.multiple_of(meta[2 * rows + pieces + q] * depth, 128)
                part = a_ref[:, pl.ds(start, depth)]
                top = part.astype(jnp.bfloat16)
                rest = (part - top.astype(jnp.float32)).astype(jnp.bfloat16)
                dot = functools.partial(jnp.dot, preferred_element_type=jnp.float32)
                out_ref[0] += dot(top, high[q]) + (dot(top, low[q]) + dot(rest, high[q]))


def half_product(ancestor, pieces, row_flags, row_blocks, piece_flags, piece_places):
    rows, count = row_flags.shape[0], len(pieces)
    depth, width = pieces[0].shape
    fetch = jnp.maximum(lax.cummax(jnp.where(row_flags > 0, row_blocks, -1)), 0)
    meta = jnp.concatenate([fetch, row_flags, piece_flags, piece_places]).astype(jnp.int32)
    return pl.pallas_call(
        functools.partial(product_kernel, rows, count),
        out_shape=jax.ShapeDtypeStruct((rows, depth, width), jnp.float32),
        grid_spec=pltpu.PrefetchScalarGridSpec(
            num_scalar_prefetch=1,
            grid=(rows,),
            in_specs=[pl.BlockSpec((depth, ancestor.shape[1]), lambda i, m: (m[i], 0))]
            + [pl.BlockSpec((depth, width), lambda i, m: (0, 0))] * count,
            out_specs=pl.BlockSpec((1, depth, width), lambda i, m: (i, 0, 0)),
            scratch_shapes=[pltpu.VMEM((count, depth, width), jnp.bfloat16)] * 2,
        ),
        cost_estimate=pl.CostEstimate(
            flops=3 * rows * depth * ancestor.shape[1] * width,
            bytes_accessed=2 * rows * depth * ancestor.shape[1],
            transcendentals=0,
        ),
        compiler_params=pltpu.CompilerParams(vmem_limit_bytes=40 * 2**20),
    )(meta, ancestor, *pieces)


def per_device(ancestor, factor, diag_inverse, structure):
    z, c = lax.axis_index("row"), lax.axis_index("col")
    depth_z, width_c = lax.axis_size("row"), lax.axis_size("col")
    ratio = width_c // depth_z
    shard = factor.shape[1]
    col_bits = width_c.bit_length() - 1
    z_bits = depth_z.bit_length() - 1

    def across(value, bit):
        pairs = [(i, i ^ (1 << bit)) for i in range(width_c)]
        return lax.ppermute(value, "col", pairs)

    def gather_along_rows(own):
        up, down = [own], [own]
        for _ in range(depth_z - 1):
            up.append(lax.ppermute(up[-1], "row", [(i, i + 1) for i in range(depth_z - 1)]))
            down.append(lax.ppermute(down[-1], "row", [(i + 1, i) for i in range(depth_z - 1)]))
        slots = [own]
        for s in range(1, depth_z):
            slots.append(jnp.where(z >= s, up[s], down[depth_z - s]))
        return jnp.stack(slots)

    def to_columns(slots):
        got = []
        for q in range(depth_z):
            plane = (c % depth_z - q) % depth_z
            value = lax.dynamic_index_in_dim(slots, (z - plane) % depth_z, 0, keepdims=False)
            pairs = []
            for d in range(width_c):
                pairs.append(((d % ratio) * depth_z + (d // ratio + q) % depth_z, d))
            got.append(lax.ppermute(value, "col", pairs))
        return got

    def keep_and_send(value, bit, place):
        shape = value.shape
        split = value.reshape((-1, 2, 2**place) + shape[1:])
        mine = (c >> bit) & 1
        keep = lax.dynamic_index_in_dim(split, mine, 1, keepdims=False)
        send = lax.dynamic_index_in_dim(split, 1 - mine, 1, keepdims=False)
        return keep.reshape((-1,) + shape[1:]), send.reshape((-1,) + shape[1:])

    def scatter_rest(value, order):
        left = list(range(1, col_bits))
        for bit in order:
            keep, send = keep_and_send(value, bit, left.index(bit))
            left.remove(bit)
            value = keep + across(send, bit)
        return value[0]

    def sum_everywhere(value):
        for bit in range(col_bits):
            halves = value.reshape((2, -1) + value.shape[1:])
            mine = (c >> bit) & 1
            keep = lax.dynamic_index_in_dim(halves, mine, 0, keepdims=False)
            send = lax.dynamic_index_in_dim(halves, 1 - mine, 0, keepdims=False)
            value = keep + across(send, bit)
        for bit in range(z_bits):
            pairs = [(i, i ^ (1 << bit)) for i in range(depth_z)]
            value = value + lax.ppermute(value, "row", pairs)
        for bit in reversed(range(col_bits)):
            other = across(value, bit)
            odd = ((c >> bit) & 1) > 0
            value = jnp.concatenate([jnp.where(odd, other, value), jnp.where(odd, value, other)])
        return value

    core = c & 1
    halves = jnp.arange(width_c // 2, dtype=jnp.int32) * 2
    places = (c // ratio + jnp.arange(depth_z, dtype=jnp.int32)) % depth_z
    piece_tiles = (c * ancestor.shape[1] + places * shard) // TILE
    piece_table = tile_table(structure, piece_tiles)

    def rows_of(parity):
        blocks = halves + parity
        return blocks, tile_table(structure, (z * ancestor.shape[0] + blocks * shard) // TILE)

    keep_blocks, keep_table = rows_of(core)
    send_blocks, send_table = rows_of(1 - core)

    slots = [gather_along_rows(factor[k]) for k in range(2)]
    pieces = [to_columns(slots[k]) for k in range(2)]
    panels, diags = [], []
    for k in range(2):
        sent = half_product(ancestor, pieces[k], send_table[k], send_blocks, piece_table[k], places)
        arrived = across(sent, 0)
        kept = half_product(ancestor, pieces[k], keep_table[k], keep_blocks, piece_table[k], places)
        middle = kept.shape[2] // 2
        total = kept + arrived
        left = scatter_rest(total[:, :, :middle], range(1, col_bits))
        right = scatter_rest(total[:, :, middle:], reversed(range(1, col_bits)))
        panel = jnp.concatenate([left, right], axis=1)
        share = lax.dot_general(
            factor[k], panel, (((0,), (0,)), ((), ())),
            precision=lax.Precision.HIGHEST, preferred_element_type=jnp.float32,
        )
        panels.append(-panel)
        diags.append(diag_inverse[k] + sum_everywhere(share))
    return jnp.stack(panels), jnp.stack(diags)


def solution(mesh):
    in_specs = (P("row", "col"), P(None, ("row", "col"), None), P(), P())
    out_specs = (P(None, ("row", "col"), None), P())
    return jax.shard_map(
        per_device, mesh=mesh, in_specs=in_specs, out_specs=out_specs, check_vma=False
    )
```

time: 829 us -> 412 us (0.50)
  waiting for transfers between devices: 660 us -> 225 us
  starting transfers between devices: 0.34 us -> 86.9 us
  matrix products: 90 us -> 3.77 us
  Pallas kernels: 0 us -> 51.1 us
  between operations: 13.9 us -> 1.75 us
    psum x2 -> x0, waiting for transfers between devices: 418 us -> none  [the longest x1 288 us: from_root(): return lax.psum(block, axis)]
    ppermute x0 -> x46, waiting for transfers between devices: none -> 225 us  [the longest x22 81.6 us: across(): return lax.ppermute(value, 'col', pairs)]
    reduce_scatter x1 -> x0, waiting for transfers between devices: 148 us -> none  [per_device(): lax.psum_scatter(partial_value, 'col', scatter_dimension=1, tiled=True)]
    all_gather x1 -> x0, waiting for transfers between devices: 94.3 us -> none  [per_device(): grouped = lax.all_gather(factor, 'col', axis=1, tiled=True)]
    ppermute x0 -> x46, starting transfers between devices: none -> 86.9 us  [the longest x6 27.6 us: gather_along_rows(): lax.ppermute(up[-1], 'row', [(i, i + 1) for i in range(depth_z - 1)])]
    dot_general x6 -> x2, matrix products: 90 us -> 3.77 us  [per_device(): lax.dot_general(factor[k], panel, (((0,), (0,)), ((), ())), precision=lax...]
    pallas_call x0 -> x4, Pallas kernels: none -> 51.1 us  [half_product(): pl.pallas_call(functools.partial(product_kernel, rows, count), out_shape=...]
    dynamic_update_slice x8 -> x0, local copies, waits for them, and re-layouts: 11.8 us -> none  [panel_product(): stacked = lax.map(one_tile, (blocks, tile_flags))]
  transfers between devices with their start and end apart: 4 -> 46, of which waited for: 4 -> 24; matrix products, arithmetic and copies ran while one was open for 1% -> 9% of each run, Pallas kernels for 0% -> 12%
where the time goes in v1:
time: 412 us; the launch traced here: 411 us
  waiting for transfers between devices  225 us (55%)
  starting transfers between devices  86.9 us (21%)
  Pallas kernels  51.1 us (12%)
  other arithmetic  25.2 us (6%)
  local copies, waits for them, and re-layouts  18.2 us (4%)
    ppermute x22, waiting for transfers between devices, across(): return lax.ppermute(value, 'col', pairs)  81.6 us
    ppermute x6, waiting for transfers between devices, gather_along_rows(): lax.ppermute(up[-1], 'row', [(i, i + 1) for i in range(depth_z - 1)])  80.4 us
    pallas_call x4, Pallas kernels, half_product(): pl.pallas_call(functools.partial(product_kernel, rows, count), out_shape=...  51.1 us
    ppermute x8, waiting for transfers between devices, to_columns(): got.append(lax.ppermute(value, 'col', pairs))  48.3 us
    ppermute x6, starting transfers between devices, gather_along_rows(): lax.ppermute(up[-1], 'row', [(i, i + 1) for i in range(depth_z - 1)])  27.6 us
    ppermute x8, starting transfers between devices, to_columns(): got.append(lax.ppermute(value, 'col', pairs))  25.8 us
    ppermute x22, starting transfers between devices, across(): return lax.ppermute(value, 'col', pairs)  25.3 us
    ppermute x4, waiting for transfers between devices, sum_everywhere(): value = value + lax.ppermute(value, 'row', pairs)  9.76 us
  transfers between devices with their start and end apart: 46, of which 24 were waited for; matrix products, arithmetic and copies ran while one was open for 9% of the time, Pallas kernels for 12%

profile of v1, /device:TPU:1, one launch (start us, length us, event | category | flops | bytes accessed | tf_op | source)
XLA Modules:
  0.0 411.5 jit_solution(14798173082620890586)
XLA Ops:
  0.6 3.5 fusion.19
  4.2 5.0 %collective-permute-start.15 = (f32[512,512]{1,0:T(8,128)}, f32[512,512]{1,0:T(8,128)}, u32[]{:S(2)}, u32[]{:S(2)}) collective-permute-start(f32[512,512]{1,0:T(8,128)} %get-tuple-element.21), channel_id=1, source_target_pairs={{0,8},{8,16},{16,24},{1,9},{9,17},{17,25},{2,10},{10,18},{18,26},{... | collective-permute-start | bytes 3145736 | tf_op jit(solution)/shard_map/ppermute | solution.py:87
  10.5 4.1 collective-permute-start
  15.9 14.5 %collective-permute-done.15 = f32[512,512]{1,0:T(8,128)} collective-permute-done((f32[512,512]{1,0:T(8,128)}, f32[512,512]{1,0:T(8,128)}, u32[]{:S(2)}, u32[]{:S(2)}) %collective-permute-start.15) | collective-permute-done | bytes 1048608 | tf_op jit(solution)/shard_map/ppermute | solution.py:87
  30.3 5.1 %collective-permute-start.19 = (f32[512,512]{1,0:T(8,128)}, f32[512,512]{1,0:T(8,128)}, u32[]{:S(2)}, u32[]{:S(2)}) collective-permute-start(f32[512,512]{1,0:T(8,128)} %collective-permute-done.15), channel_id=1, source_target_pairs={{0,8},{8,16},{16,24},{1,9},{9,17},{17,25},{2,10},{10,18},{18,26},{... | collective-permute-start | bytes 3145736 | tf_op jit(solution)/shard_map/ppermute | solution.py:87
  37.3 15.5 %collective-permute-done = f32[512,512]{1,0:T(8,128)S(1)} collective-permute-done((f32[512,512]{1,0:T(8,128)}, f32[512,512]{1,0:T(8,128)S(1)}, u32[]{:S(2)}, u32[]{:S(2)}) %collective-permute-start) | collective-permute-done | bytes 1048608 | tf_op jit(solution)/shard_map/ppermute | solution.py:87
  52.8 5.0 %collective-permute-start.4 = (f32[512,512]{1,0:T(8,128)S(1)}, f32[512,512]{1,0:T(8,128)}, u32[]{:S(2)}, u32[]{:S(2)}) collective-permute-start(f32[512,512]{1,0:T(8,128)S(1)} %collective-permute-done), channel_id=1, source_target_pairs={{0,8},{8,16},{16,24},{1,9},{9,17},{17,25},{2,10},{10,18},{18,26},{... | collective-permute-start | bytes 3145736 | tf_op jit(solution)/shard_map/ppermute | solution.py:87
  59.8 15.5 %collective-permute-done.19 = f32[512,512]{1,0:T(8,128)} collective-permute-done((f32[512,512]{1,0:T(8,128)}, f32[512,512]{1,0:T(8,128)}, u32[]{:S(2)}, u32[]{:S(2)}) %collective-permute-start.19) | collective-permute-done | bytes 1048608 | tf_op jit(solution)/shard_map/ppermute | solution.py:87
  75.3 4.2 %collective-permute-start.20 = (f32[512,512]{1,0:T(8,128)}, f32[512,512]{1,0:T(8,128)S(1)}, u32[]{:S(2)}, u32[]{:S(2)}) collective-permute-start(f32[512,512]{1,0:T(8,128)} %collective-permute-done.19), channel_id=1, source_target_pairs={{0,8},{8,16},{16,24},{1,9},{9,17},{17,25},{2,10},{10,18},{18,26},{... | collective-permute-start | bytes 3145736 | tf_op jit(solution)/shard_map/ppermute | solution.py:87
  81.4 16.3 %collective-permute-done.4 = f32[512,512]{1,0:T(8,128)} collective-permute-done((f32[512,512]{1,0:T(8,128)S(1)}, f32[512,512]{1,0:T(8,128)}, u32[]{:S(2)}, u32[]{:S(2)}) %collective-permute-start.4) | collective-permute-done | bytes 1048608 | tf_op jit(solution)/shard_map/ppermute | solution.py:87
  97.6 4.3 %collective-permute-start.5 = (f32[512,512]{1,0:T(8,128)}, f32[512,512]{1,0:T(8,128)S(1)}, u32[]{:S(2)}, u32[]{:S(2)}) collective-permute-start(f32[512,512]{1,0:T(8,128)} %collective-permute-done.4), channel_id=1, source_target_pairs={{0,8},{8,16},{16,24},{1,9},{9,17},{17,25},{2,10},{10,18},{18,26},{... | collective-permute-start | bytes 3145736 | tf_op jit(solution)/shard_map/ppermute | solution.py:87
  105.3 14.9 %collective-permute-done.20 = f32[512,512]{1,0:T(8,128)S(1)} collective-permute-done((f32[512,512]{1,0:T(8,128)}, f32[512,512]{1,0:T(8,128)S(1)}, u32[]{:S(2)}, u32[]{:S(2)}) %collective-permute-start.20) | collective-permute-done | bytes 1048608 | tf_op jit(solution)/shard_map/ppermute | solution.py:87
  121.7 3.2 collective-permute-done.18
  126.3 6.5 %collective-permute-start.21 = (f32[512,512]{1,0:T(8,128)S(1)}, f32[512,512]{1,0:T(8,128)S(1)}, u32[]{:S(2)}, u32[]{:S(2)}) collective-permute-start(f32[512,512]{1,0:T(8,128)S(1)} %get-tuple-element.16), channel_id=1, source_target_pairs={{0,0},{4,1},{1,2},{5,3},{2,4},{6,5},{3,6},{7,7},{8,8},{12,9},{9,10... | collective-permute-start | bytes 3145736 | tf_op jit(solution)/shard_map/ppermute | solution.py:102
  132.7 1.9 collective-permute-start.22
  134.7 2.7 collective-permute-start.23
  138.9 3.8 collective-permute-done.5
  142.7 4.6 %collective-permute-start.24 = (f32[512,512]{1,0:T(8,128)S(1)}, f32[512,512]{1,0:T(8,128)S(1)}, u32[]{:S(2)}, u32[]{:S(2)}) collective-permute-start(f32[512,512]{1,0:T(8,128)S(1)} %get-tuple-element.13), channel_id=1, source_target_pairs={{3,0},{7,1},{0,2},{4,3},{1,4},{5,5},{2,6},{6,7},{11,8},{15,9},{8,1... | collective-permute-start | bytes 3145736 | tf_op jit(solution)/shard_map/ppermute | solution.py:102
  149.6 3.8 collective-permute-start.6
  153.4 1.9 collective-permute-start.7
  155.3 25.7 %collective-permute-done.22.refs_1_ = f32[512,512]{1,0:T(8,128)S(1)} collective-permute-done((f32[512,512]{1,0:T(8,128)S(1)}, f32[512,512]{1,0:T(8,128)S(1)}, u32[]{:S(2)}, u32[]{:S(2)}) %collective-permute-start.22) | collective-permute-done | bytes 1048608 | tf_op jit(solution)/shard_map/ppermute | solution.py:102
  182.7 2.7 collective-permute-start.9
  185.6 16.4 %shard_map.62 = f32[4,512,512]{2,1,0:T(8,128)} custom-call(s32[16]{0:T(128)S(1)} %get-tuple-element.47.meta, f32[4096,2048]{1,0:T(8,128)} %a_ref.7, f32[512,512]{1,0:T(8,128)S(1)} %collective-permute-done.21.refs_0_, f32[512,512]{1,0:T(8,128)S(1)} %collective-permute-done.22.refs_1_, f32[512,512]{1,0:T(8,128)S(1)} %collective-permute-done.23.refs_2_, ...), custom_call_target="tpu_custom_call" | custom-call | flops 6442450944 | bytes 8388608 | tf_op jit(solution)/shard_map/pallas_call | solution.py:52
  202.1 22.6 %collective-permute-done.8.refs_2_ = f32[512,512]{1,0:T(8,128)S(1)} collective-permute-done((f32[512,512]{1,0:T(8,128)S(1)}, f32[512,512]{1,0:T(8,128)S(1)}, u32[]{:S(2)}, u32[]{:S(2)}) %collective-permute-start.8) | collective-permute-done | bytes 1048608 | tf_op jit(solution)/shard_map/ppermute | solution.py:102
  224.7 9.7 %shard_map.60 = f32[4,512,512]{2,1,0:T(8,128)} custom-call(s32[16]{0:T(128)S(1)} %get-tuple-element.35.meta, f32[4096,2048]{1,0:T(8,128)} %a_ref.7, f32[512,512]{1,0:T(8,128)S(1)} %collective-permute-done.6.refs_0_, f32[512,512]{1,0:T(8,128)S(1)} %collective-permute-done.7.refs_1_, f32[512,512]{1,0:T(8,128)S(1)} %collective-permute-done.8.refs_2_, ...), custom_call_target="tpu_custom_call" | custom-call | flops 6442450944 | bytes 8388608 | tf_op jit(solution)/shard_map/pallas_call | solution.py:52
  234.4 3.3 collective-permute-start.10
  239.0 15.0 %shard_map.61 = f32[4,512,512]{2,1,0:T(8,128)S(1)} custom-call(s32[16]{0:T(128)S(1)} %get-tuple-element.48.meta, f32[4096,2048]{1,0:T(8,128)} %a_ref.7, f32[512,512]{1,0:T(8,128)S(1)} %collective-permute-done.21.refs_0_, f32[512,512]{1,0:T(8,128)S(1)} %collective-permute-done.22.refs_1_, f32[512,512]{1,0:T(8,128)S(1)} %collective-permute-done.23.refs_2_, ...), custom_call_target="tpu_custom_call" | custom-call | flops 6442450944 | bytes 8388608 | tf_op jit(solution)/shard_map/pallas_call | solution.py:52
  254.0 10.0 %shard_map.59 = f32[4,512,512]{2,1,0:T(8,128)S(1)} custom-call(s32[16]{0:T(128)S(1)} %get-tuple-element.36.meta, f32[4096,2048]{1,0:T(8,128)} %a_ref.7, f32[512,512]{1,0:T(8,128)S(1)} %copy-done.3, f32[512,512]{1,0:T(8,128)S(1)} %copy-done.5, f32[512,512]{1,0:T(8,128)S(1)} %copy-done.7, f32[512,512]{1,0:T(8,128)S(1)} %copy-done.9), custom_call_target="tpu_custom_call" | custom-call | flops 6442450944 | bytes 8388608 | tf_op jit(solution)/shard_map/pallas_call | solution.py:52
  264.0 3.2 add.332
  267.8 3.8 add.323
  271.6 1.8 fusion.17
  276.6 2.3 dynamic-slice_bitcast_fusion.7
  280.5 12.6 %collective-permute-done.28 = f32[2,512,256]{2,1,0:T(8,128)} collective-permute-done((f32[2,512,256]{2,1,0:T(8,128)S(1)}, f32[2,512,256]{2,1,0:T(8,128)}, u32[]{:S(2)}, u32[]{:S(2)}) %collective-permute-start.28) | collective-permute-done | bytes 1048608 | tf_op jit(solution)/shard_map/ppermute | solution.py:82
  294.6 19.2 %collective-permute-done.13 = f32[2,512,256]{2,1,0:T(8,128)} collective-permute-done((f32[2,512,256]{2,1,0:T(8,128)}, f32[2,512,256]{2,1,0:T(8,128)}, u32[]{:S(2)}, u32[]{:S(2)}) %collective-permute-start.13) | collective-permute-done | bytes 1048608 | tf_op jit(solution)/shard_map/ppermute | solution.py:82
  316.9 9.9 %collective-permute-done.26 = f32[2,512,256]{2,1,0:T(8,128)S(1)} collective-permute-done((f32[2,512,256]{2,1,0:T(8,128)S(1)}, f32[2,512,256]{2,1,0:T(8,128)S(1)}, u32[]{:S(2)}, u32[]{:S(2)}) %collective-permute-start.26) | collective-permute-done | bytes 1048608 | tf_op jit(solution)/shard_map/ppermute | solution.py:82
  327.7 20.3 %collective-permute-done.14 = f32[1,512,256]{2,1,0:T(8,128)S(1)} collective-permute-done((f32[1,512,256]{2,1,0:T(8,128)S(1)}, f32[1,512,256]{2,1,0:T(8,128)S(1)}, u32[]{:S(2)}, u32[]{:S(2)}) %collective-permute-start.14) | collective-permute-done | bytes 524320 | tf_op jit(solution)/shard_map/ppermute | solution.py:82
  348.1 1.9 fusion
  351.0 1.9 fusion.4
  359.2 5.2 %collective-permute-done.31 = f32[128,512]{1,0:T(8,128)S(1)} collective-permute-done((f32[128,512]{1,0:T(8,128)S(1)}, f32[128,512]{1,0:T(8,128)S(1)}, u32[]{:S(2)}, u32[]{:S(2)}) %collective-permute-start.31) | collective-permute-done | bytes 262176 | tf_op jit(solution)/shard_map/ppermute | solution.py:82
  364.9 5.2 %collective-permute-done.39 = f32[128,512]{1,0:T(8,128)S(1)} collective-permute-done((f32[128,512]{1,0:T(8,128)S(1)}, f32[128,512]{1,0:T(8,128)S(1)}, u32[]{:S(2)}, u32[]{:S(2)}) %collective-permute-start.39) | collective-permute-done | bytes 262176 | tf_op jit(solution)/shard_map/ppermute | solution.py:82
  370.6 3.8 collective-permute-done.40
  375.0 4.7 %collective-permute-done.41 = f32[64,512]{1,0:T(8,128)S(1)} collective-permute-done((f32[64,512]{1,0:T(8,128)S(1)}, f32[64,512]{1,0:T(8,128)S(1)}, u32[]{:S(2)}, u32[]{:S(2)}) %collective-permute-start.41) | collective-permute-done | bytes 131104 | tf_op jit(solution)/shard_map/ppermute | solution.py:130
  379.8 1.7 collective-permute-done.34
  381.5 4.1 collective-permute-start.35
  385.8 3.2 collective-permute-done.42
  390.0 4.5 %collective-permute-done.43 = f32[64,512]{1,0:T(8,128)S(1)} collective-permute-done((f32[64,512]{1,0:T(8,128)S(1)}, f32[64,512]{1,0:T(8,128)S(1)}, u32[]{:S(2)}, u32[]{:S(2)}) %collective-permute-start.43) | collective-permute-done | bytes 131104 | tf_op jit(solution)/shard_map/ppermute | solution.py:82
  395.5 7.9 %collective-permute-start.37 = (f32[256,512]{1,0:T(8,128)S(1)}, f32[256,512]{1,0:T(8,128)S(1)}, u32[]{:S(2)}, u32[]{:S(2)}) collective-permute-start(f32[256,512]{1,0:T(8,128)S(1)} %pad_maximum_fusion.4), channel_id=1, source_target_pairs={{0,1},{1,0},{2,3},{3,2},{4,5},{5,4},{6,7},{7,6},{8,9},{9,8},{10,11... | collective-permute-start | bytes 1572872 | tf_op jit(solution)/shard_map/ppermute | solution.py:82
  403.6 2.7 collective-permute-start.45
  (183 shorter events, 48.3 us)
Async XLA Ops:
  4.2 26.2 %collective-permute-start.15 = (f32[512,512]{1,0:T(8,128)}, f32[512,512]{1,0:T(8,128)}, u32[]{:S(2)}, u32[]{:S(2)}) collective-permute-start(f32[512,512]{1,0:T(8,128)} %get-tuple-element.21), channel_id=1, source_target_pairs={{0,8},{8,16},{16,24},{1,9},{9,17},{17,25},{2,10},{10,18},{18,26},{... | collective-permute-start | bytes 3145736 | tf_op jit(solution)/shard_map/ppermute | solution.py:87
  9.2 26.3 %collective-permute-start.16 = (f32[512,512]{1,0:T(8,128)}, f32[512,512]{1,0:T(8,128)}, u32[]{:S(2)}, u32[]{:S(2)}) collective-permute-start(f32[512,512]{1,0:T(8,128)} %get-tuple-element.21), channel_id=1, source_target_pairs={{8,0},{16,8},{24,16},{9,1},{17,9},{25,17},{10,2},{18,10},{26,18},{... | collective-permute-start | bytes 3145736 | tf_op jit(solution)/shard_map/ppermute | solution.py:88
  10.5 42.3 %collective-permute-start = (f32[512,512]{1,0:T(8,128)}, f32[512,512]{1,0:T(8,128)S(1)}, u32[]{:S(2)}, u32[]{:S(2)}) collective-permute-start(f32[512,512]{1,0:T(8,128)} %get-tuple-element.20), channel_id=1, source_target_pairs={{0,8},{8,16},{16,24},{1,9},{9,17},{17,25},{2,10},{10,18},{18,26},{... | collective-permute-start | bytes 3145736 | tf_op jit(solution)/shard_map/ppermute | solution.py:87
  14.5 43.2 %collective-permute-start.1 = (f32[512,512]{1,0:T(8,128)}, f32[512,512]{1,0:T(8,128)S(1)}, u32[]{:S(2)}, u32[]{:S(2)}) collective-permute-start(f32[512,512]{1,0:T(8,128)} %get-tuple-element.20), channel_id=1, source_target_pairs={{8,0},{16,8},{24,16},{9,1},{17,9},{25,17},{10,2},{18,10},{26,18},{... | collective-permute-start | bytes 3145736 | tf_op jit(solution)/shard_map/ppermute | solution.py:88
  30.3 44.9 %collective-permute-start.19 = (f32[512,512]{1,0:T(8,128)}, f32[512,512]{1,0:T(8,128)}, u32[]{:S(2)}, u32[]{:S(2)}) collective-permute-start(f32[512,512]{1,0:T(8,128)} %collective-permute-done.15), channel_id=1, source_target_pairs={{0,8},{8,16},{16,24},{1,9},{9,17},{17,25},{2,10},{10,18},{18,26},{... | collective-permute-start | bytes 3145736 | tf_op jit(solution)/shard_map/ppermute | solution.py:87
  35.5 44.6 %collective-permute-start.17 = (f32[512,512]{1,0:T(8,128)}, f32[512,512]{1,0:T(8,128)}, u32[]{:S(2)}, u32[]{:S(2)}) collective-permute-start(f32[512,512]{1,0:T(8,128)} %collective-permute-done.16), channel_id=1, source_target_pairs={{8,0},{16,8},{24,16},{9,1},{17,9},{25,17},{10,2},{18,10},{26,18},{... | collective-permute-start | bytes 3145736 | tf_op jit(solution)/shard_map/ppermute | solution.py:88
  52.8 68.9 %copy-start.20 = (f32[512,512]{1,0:T(8,128)}, f32[512,512]{1,0:T(8,128)S(1)}, u32[]{:S(2)}) copy-start(f32[512,512]{1,0:T(8,128)S(1)} %collective-permute-done) | copy-start | bytes 3145732
  52.8 44.8 %collective-permute-start.4 = (f32[512,512]{1,0:T(8,128)S(1)}, f32[512,512]{1,0:T(8,128)}, u32[]{:S(2)}, u32[]{:S(2)}) collective-permute-start(f32[512,512]{1,0:T(8,128)S(1)} %collective-permute-done), channel_id=1, source_target_pairs={{0,8},{8,16},{16,24},{1,9},{9,17},{17,25},{2,10},{10,18},{18,26},{... | collective-permute-start | bytes 3145736 | tf_op jit(solution)/shard_map/ppermute | solution.py:87
  57.8 63.9 %copy-start.22 = (f32[512,512]{1,0:T(8,128)}, f32[512,512]{1,0:T(8,128)S(1)}, u32[]{:S(2)}) copy-start(f32[512,512]{1,0:T(8,128)S(1)} %collective-permute-done.1) | copy-start | bytes 3145732
  57.8 44.7 %collective-permute-start.2 = (f32[512,512]{1,0:T(8,128)S(1)}, f32[512,512]{1,0:T(8,128)}, u32[]{:S(2)}, u32[]{:S(2)}) collective-permute-start(f32[512,512]{1,0:T(8,128)S(1)} %collective-permute-done.1), channel_id=1, source_target_pairs={{8,0},{16,8},{24,16},{9,1},{17,9},{25,17},{10,2},{18,10},{26,18},{... | collective-permute-start | bytes 3145736 | tf_op jit(solution)/shard_map/ppermute | solution.py:88
  75.3 44.9 %collective-permute-start.20 = (f32[512,512]{1,0:T(8,128)}, f32[512,512]{1,0:T(8,128)S(1)}, u32[]{:S(2)}, u32[]{:S(2)}) collective-permute-start(f32[512,512]{1,0:T(8,128)} %collective-permute-done.19), channel_id=1, source_target_pairs={{0,8},{8,16},{16,24},{1,9},{9,17},{17,25},{2,10},{10,18},{18,26},{... | collective-permute-start | bytes 3145736 | tf_op jit(solution)/shard_map/ppermute | solution.py:87
  80.0 44.8 %collective-permute-start.18 = (f32[512,512]{1,0:T(8,128)}, f32[512,512]{1,0:T(8,128)S(1)}, u32[]{:S(2)}, u32[]{:S(2)}) collective-permute-start(f32[512,512]{1,0:T(8,128)} %collective-permute-done.17), channel_id=1, source_target_pairs={{8,0},{16,8},{24,16},{9,1},{17,9},{25,17},{10,2},{18,10},{26,18},{... | collective-permute-start | bytes 3145736 | tf_op jit(solution)/shard_map/ppermute | solution.py:88
  97.6 45.0 %collective-permute-start.5 = (f32[512,512]{1,0:T(8,128)}, f32[512,512]{1,0:T(8,128)S(1)}, u32[]{:S(2)}, u32[]{:S(2)}) collective-permute-start(f32[512,512]{1,0:T(8,128)} %collective-permute-done.4), channel_id=1, source_target_pairs={{0,8},{8,16},{16,24},{1,9},{9,17},{17,25},{2,10},{10,18},{18,26},{... | collective-permute-start | bytes 3145736 | tf_op jit(solution)/shard_map/ppermute | solution.py:87
  102.5 45.0 %collective-permute-start.3 = (f32[512,512]{1,0:T(8,128)}, f32[512,512]{1,0:T(8,128)S(1)}, u32[]{:S(2)}, u32[]{:S(2)}) collective-permute-start(f32[512,512]{1,0:T(8,128)} %collective-permute-done.2), channel_id=1, source_target_pairs={{8,0},{16,8},{24,16},{9,1},{17,9},{25,17},{10,2},{18,10},{26,18},{... | collective-permute-start | bytes 3145736 | tf_op jit(solution)/shard_map/ppermute | solution.py:88
  126.3 27.1 %collective-permute-start.21 = (f32[512,512]{1,0:T(8,128)S(1)}, f32[512,512]{1,0:T(8,128)S(1)}, u32[]{:S(2)}, u32[]{:S(2)}) collective-permute-start(f32[512,512]{1,0:T(8,128)S(1)} %get-tuple-element.16), channel_id=1, source_target_pairs={{0,0},{4,1},{1,2},{5,3},{2,4},{6,5},{3,6},{7,7},{8,8},{12,9},{9,10... | collective-permute-start | bytes 3145736 | tf_op jit(solution)/shard_map/ppermute | solution.py:102
  132.7 48.3 %collective-permute-start.22 = (f32[512,512]{1,0:T(8,128)S(1)}, f32[512,512]{1,0:T(8,128)S(1)}, u32[]{:S(2)}, u32[]{:S(2)}) collective-permute-start(f32[512,512]{1,0:T(8,128)S(1)} %get-tuple-element.15), channel_id=1, source_target_pairs={{1,0},{5,1},{2,2},{6,3},{3,4},{7,5},{0,6},{4,7},{9,8},{13,9},{10,1... | collective-permute-start | bytes 3145736 | tf_op jit(solution)/shard_map/ppermute | solution.py:102
  134.7 48.0 %collective-permute-start.23 = (f32[512,512]{1,0:T(8,128)S(1)}, f32[512,512]{1,0:T(8,128)S(1)}, u32[]{:S(2)}, u32[]{:S(2)}) collective-permute-start(f32[512,512]{1,0:T(8,128)S(1)} %get-tuple-element.14), channel_id=1, source_target_pairs={{2,0},{6,1},{3,2},{7,3},{0,4},{4,5},{1,6},{5,7},{10,8},{14,9},{11,... | collective-permute-start | bytes 3145736 | tf_op jit(solution)/shard_map/ppermute | solution.py:102
  142.7 42.9 %collective-permute-start.24 = (f32[512,512]{1,0:T(8,128)S(1)}, f32[512,512]{1,0:T(8,128)S(1)}, u32[]{:S(2)}, u32[]{:S(2)}) collective-permute-start(f32[512,512]{1,0:T(8,128)S(1)} %get-tuple-element.13), channel_id=1, source_target_pairs={{3,0},{7,1},{0,2},{4,3},{1,4},{5,5},{2,6},{6,7},{11,8},{15,9},{8,1... | collective-permute-start | bytes 3145736 | tf_op jit(solution)/shard_map/ppermute | solution.py:102
  149.6 52.4 %collective-permute-start.6 = (f32[512,512]{1,0:T(8,128)S(1)}, f32[512,512]{1,0:T(8,128)S(1)}, u32[]{:S(2)}, u32[]{:S(2)}) collective-permute-start(f32[512,512]{1,0:T(8,128)S(1)} %get-tuple-element.10), channel_id=1, source_target_pairs={{0,0},{4,1},{1,2},{5,3},{2,4},{6,5},{3,6},{7,7},{8,8},{12,9},{9,10... | collective-permute-start | bytes 3145736 | tf_op jit(solution)/shard_map/ppermute | solution.py:102
  153.4 48.7 %collective-permute-start.7 = (f32[512,512]{1,0:T(8,128)S(1)}, f32[512,512]{1,0:T(8,128)S(1)}, u32[]{:S(2)}, u32[]{:S(2)}) collective-permute-start(f32[512,512]{1,0:T(8,128)S(1)} %get-tuple-element.9), channel_id=1, source_target_pairs={{1,0},{5,1},{2,2},{6,3},{3,4},{7,5},{0,6},{4,7},{9,8},{13,9},{10,1... | collective-permute-start | bytes 3145736 | tf_op jit(solution)/shard_map/ppermute | solution.py:102
  181.0 43.6 %collective-permute-start.8 = (f32[512,512]{1,0:T(8,128)S(1)}, f32[512,512]{1,0:T(8,128)S(1)}, u32[]{:S(2)}, u32[]{:S(2)}) collective-permute-start(f32[512,512]{1,0:T(8,128)S(1)} %get-tuple-element.8), channel_id=1, source_target_pairs={{2,0},{6,1},{3,2},{7,3},{0,4},{4,5},{1,6},{5,7},{10,8},{14,9},{11,... | collective-permute-start | bytes 3145736 | tf_op jit(solution)/shard_map/ppermute | solution.py:102
  182.7 42.0 %collective-permute-start.9 = (f32[512,512]{1,0:T(8,128)S(1)}, f32[512,512]{1,0:T(8,128)S(1)}, u32[]{:S(2)}, u32[]{:S(2)}) collective-permute-start(f32[512,512]{1,0:T(8,128)S(1)} %get-tuple-element.7), channel_id=1, source_target_pairs={{3,0},{7,1},{0,2},{4,3},{1,4},{5,5},{2,6},{6,7},{11,8},{15,9},{8,1... | collective-permute-start | bytes 3145736 | tf_op jit(solution)/shard_map/ppermute | solution.py:102
  202.0 62.0 %collective-permute-start.25 = (f32[4,512,512]{2,1,0:T(8,128)}, f32[4,512,512]{2,1,0:T(8,128)}, u32[]{:S(2)}, u32[]{:S(2)}) collective-permute-start(f32[4,512,512]{2,1,0:T(8,128)} %shard_map.62), channel_id=1, source_target_pairs={{0,1},{1,0},{2,3},{3,2},{4,5},{5,4},{6,7},{7,6},{8,9},{9,8},{10,11... | collective-permute-start | bytes 12582920 | tf_op jit(solution)/shard_map/ppermute | solution.py:82
  234.4 33.4 %collective-permute-start.10 = (f32[4,512,512]{2,1,0:T(8,128)}, f32[4,512,512]{2,1,0:T(8,128)}, u32[]{:S(2)}, u32[]{:S(2)}) collective-permute-start(f32[4,512,512]{2,1,0:T(8,128)} %shard_map.60), channel_id=1, source_target_pairs={{0,1},{1,0},{2,3},{3,2},{4,5},{5,4},{6,7},{7,6},{8,9},{9,8},{10,11... | collective-permute-start | bytes 12582920 | tf_op jit(solution)/shard_map/ppermute | solution.py:82
  267.7 25.4 %collective-permute-start.28 = (f32[2,512,256]{2,1,0:T(8,128)S(1)}, f32[2,512,256]{2,1,0:T(8,128)}, u32[]{:S(2)}, u32[]{:S(2)}) collective-permute-start(f32[2,512,256]{2,1,0:T(8,128)S(1)} %dynamic-slice_bitcast_fusion), channel_id=1, source_target_pairs={{0,4},{1,5},{2,6},{3,7},{4,0},{5,1},{6,2},{7,3},{8,12},{9,13},{10,... | collective-permute-start | bytes 3145736 | tf_op jit(solution)/shard_map/ppermute | solution.py:82
  275.8 38.1 %collective-permute-start.13 = (f32[2,512,256]{2,1,0:T(8,128)}, f32[2,512,256]{2,1,0:T(8,128)}, u32[]{:S(2)}, u32[]{:S(2)}) collective-permute-start(f32[2,512,256]{2,1,0:T(8,128)} %dynamic-slice_bitcast_fusion.6), channel_id=1, source_target_pairs={{0,4},{1,5},{2,6},{3,7},{4,0},{5,1},{6,2},{7,3},{8,12},{9,13},{10,... | collective-permute-start | bytes 3145736 | tf_op jit(solution)/shard_map/ppermute | solution.py:82
  278.9 36.4 %collective-permute-start.11 = (f32[2,512,256]{2,1,0:T(8,128)}, f32[2,512,256]{2,1,0:T(8,128)}, u32[]{:S(2)}, u32[]{:S(2)}) collective-permute-start(f32[2,512,256]{2,1,0:T(8,128)} %dynamic-slice_bitcast_fusion.7), channel_id=1, source_target_pairs={{0,2},{1,3},{2,0},{3,1},{4,6},{5,7},{6,4},{7,5},{8,10},{9,11},{10,... | collective-permute-start | bytes 3145736 | tf_op jit(solution)/shard_map/ppermute | solution.py:82
  279.0 47.8 %collective-permute-start.26 = (f32[2,512,256]{2,1,0:T(8,128)S(1)}, f32[2,512,256]{2,1,0:T(8,128)S(1)}, u32[]{:S(2)}, u32[]{:S(2)}) collective-permute-start(f32[2,512,256]{2,1,0:T(8,128)S(1)} %dynamic-slice_bitcast_fusion.1), channel_id=1, source_target_pairs={{0,2},{1,3},{2,0},{3,1},{4,6},{5,7},{6,4},{7,5},{8,10},{9,11},{10,... | collective-permute-start | bytes 3145736 | tf_op jit(solution)/shard_map/ppermute | solution.py:82
  294.6 56.3 %collective-permute-start.29 = (f32[1,512,256]{2,1,0:T(8,128)S(1)}, f32[1,512,256]{2,1,0:T(8,128)S(1)}, u32[]{:S(2)}, u32[]{:S(2)}) collective-permute-start(f32[1,512,256]{2,1,0:T(8,128)S(1)} %constant_dynamic-slice_fusion), channel_id=1, source_target_pairs={{0,2},{1,3},{2,0},{3,1},{4,6},{5,7},{6,4},{7,5},{8,10},{9,11},{10,... | collective-permute-start | bytes 1572872 | tf_op jit(solution)/shard_map/ppermute | solution.py:82
  315.3 32.7 %collective-permute-start.14 = (f32[1,512,256]{2,1,0:T(8,128)S(1)}, f32[1,512,256]{2,1,0:T(8,128)S(1)}, u32[]{:S(2)}, u32[]{:S(2)}) collective-permute-start(f32[1,512,256]{2,1,0:T(8,128)S(1)} %constant_dynamic-slice_fusion.2), channel_id=1, source_target_pairs={{0,2},{1,3},{2,0},{3,1},{4,6},{5,7},{6,4},{7,5},{8,10},{9,11},{10,... | collective-permute-start | bytes 1572872 | tf_op jit(solution)/shard_map/ppermute | solution.py:82
  316.8 31.2 %collective-permute-start.12 = (f32[1,512,256]{2,1,0:T(8,128)S(1)}, f32[1,512,256]{2,1,0:T(8,128)S(1)}, u32[]{:S(2)}, u32[]{:S(2)}) collective-permute-start(f32[1,512,256]{2,1,0:T(8,128)S(1)} %constant_dynamic-slice_fusion.3), channel_id=1, source_target_pairs={{0,4},{1,5},{2,6},{3,7},{4,0},{5,1},{6,2},{7,3},{8,12},{9,13},{10,... | collective-permute-start | bytes 1572872 | tf_op jit(solution)/shard_map/ppermute | solution.py:82
  327.0 23.9 %collective-permute-start.27 = (f32[1,512,256]{2,1,0:T(8,128)S(1)}, f32[1,512,256]{2,1,0:T(8,128)S(1)}, u32[]{:S(2)}, u32[]{:S(2)}) collective-permute-start(f32[1,512,256]{2,1,0:T(8,128)S(1)} %constant_dynamic-slice_fusion.1), channel_id=1, source_target_pairs={{0,4},{1,5},{2,6},{3,7},{4,0},{5,1},{6,2},{7,3},{8,12},{9,13},{10,... | collective-permute-start | bytes 1572872 | tf_op jit(solution)/shard_map/ppermute | solution.py:82
  350.8 4.4 %collective-permute-start.30 = (f32[256,512]{1,0:T(8,128)}, f32[256,512]{1,0:T(8,128)}, u32[]{:S(2)}, u32[]{:S(2)}) collective-permute-start(f32[256,512]{1,0:T(8,128)} %dynamic-slice_bitcast_fusion.13), channel_id=1, source_target_pairs={{0,1},{1,0},{2,3},{3,2},{4,5},{5,4},{6,7},{7,6},{8,9},{9,8},{10,11... | collective-permute-start | bytes 1572872 | tf_op jit(solution)/shard_map/ppermute | solution.py:82
  354.7 2.5 collective-permute-start.38
  356.5 8.0 %collective-permute-start.31 = (f32[128,512]{1,0:T(8,128)S(1)}, f32[128,512]{1,0:T(8,128)S(1)}, u32[]{:S(2)}, u32[]{:S(2)}) collective-permute-start(f32[128,512]{1,0:T(8,128)S(1)} %dynamic-slice_bitcast_fusion.15), channel_id=1, source_target_pairs={{0,2},{1,3},{2,0},{3,1},{4,6},{5,7},{6,4},{7,5},{8,10},{9,11},{10,... | collective-permute-start | bytes 786440 | tf_op jit(solution)/shard_map/ppermute | solution.py:82
  358.3 11.7 %collective-permute-start.39 = (f32[128,512]{1,0:T(8,128)S(1)}, f32[128,512]{1,0:T(8,128)S(1)}, u32[]{:S(2)}, u32[]{:S(2)}) collective-permute-start(f32[128,512]{1,0:T(8,128)S(1)} %dynamic-slice_bitcast_fusion.14), channel_id=1, source_target_pairs={{0,2},{1,3},{2,0},{3,1},{4,6},{5,7},{6,4},{7,5},{8,10},{9,11},{10,... | collective-permute-start | bytes 786440 | tf_op jit(solution)/shard_map/ppermute | solution.py:82
  364.5 6.0 %collective-permute-start.32 = (f32[64,512]{1,0:T(8,128)S(1)}, f32[64,512]{1,0:T(8,128)S(1)}, u32[]{:S(2)}, u32[]{:S(2)}) collective-permute-start(f32[64,512]{1,0:T(8,128)S(1)} %dynamic-slice_bitcast_fusion.17), channel_id=1, source_target_pairs={{0,4},{1,5},{2,6},{3,7},{4,0},{5,1},{6,2},{7,3},{8,12},{9,13},{10,... | collective-permute-start | bytes 393224 | tf_op jit(solution)/shard_map/ppermute | solution.py:82
  370.1 4.3 %collective-permute-start.40 = (f32[64,512]{1,0:T(8,128)S(1)}, f32[64,512]{1,0:T(8,128)S(1)}, u32[]{:S(2)}, u32[]{:S(2)}) collective-permute-start(f32[64,512]{1,0:T(8,128)S(1)} %dynamic-slice_bitcast_fusion.16), channel_id=1, source_target_pairs={{0,4},{1,5},{2,6},{3,7},{4,0},{5,1},{6,2},{7,3},{8,12},{9,13},{10,... | collective-permute-start | bytes 393224 | tf_op jit(solution)/shard_map/ppermute | solution.py:82
  370.5 4.2 %collective-permute-start.33 = (f32[64,512]{1,0:T(8,128)S(1)}, f32[64,512]{1,0:T(8,128)S(1)}, u32[]{:S(2)}, u32[]{:S(2)}) collective-permute-start(f32[64,512]{1,0:T(8,128)S(1)} %bitcast_add_fusion.9), channel_id=1, source_target_pairs={{0,8},{8,0},{16,24},{24,16},{1,9},{9,1},{17,25},{25,17},{2,10},{10... | collective-permute-start | bytes 393224 | tf_op jit(solution)/shard_map/ppermute | solution.py:130
  374.5 5.3 %collective-permute-start.41 = (f32[64,512]{1,0:T(8,128)S(1)}, f32[64,512]{1,0:T(8,128)S(1)}, u32[]{:S(2)}, u32[]{:S(2)}) collective-permute-start(f32[64,512]{1,0:T(8,128)S(1)} %bitcast_add_fusion.8), channel_id=1, source_target_pairs={{0,8},{8,0},{16,24},{24,16},{1,9},{9,1},{17,25},{25,17},{2,10},{10... | collective-permute-start | bytes 393224 | tf_op jit(solution)/shard_map/ppermute | solution.py:130
  374.7 6.8 %collective-permute-start.34 = (f32[64,512]{1,0:T(8,128)S(1)}, f32[64,512]{1,0:T(8,128)S(1)}, u32[]{:S(2)}, u32[]{:S(2)}) collective-permute-start(f32[64,512]{1,0:T(8,128)S(1)} %add.342), channel_id=1, source_target_pairs={{0,16},{8,24},{16,0},{24,8},{1,17},{9,25},{17,1},{25,9},{2,18},{10... | collective-permute-start | bytes 393224 | tf_op jit(solution)/shard_map/ppermute | solution.py:130
  379.8 9.2 %collective-permute-start.42 = (f32[64,512]{1,0:T(8,128)S(1)}, f32[64,512]{1,0:T(8,128)S(1)}, u32[]{:S(2)}, u32[]{:S(2)}) collective-permute-start(f32[64,512]{1,0:T(8,128)S(1)} %add.348), channel_id=1, source_target_pairs={{0,16},{8,24},{16,0},{24,8},{1,17},{9,25},{17,1},{25,9},{2,18},{10... | collective-permute-start | bytes 393224 | tf_op jit(solution)/shard_map/ppermute | solution.py:130
  381.5 8.3 %collective-permute-start.35 = (f32[64,512]{1,0:T(8,128)S(1)}, f32[64,512]{1,0:T(8,128)S(1)}, u32[]{:S(2)}, u32[]{:S(2)}) collective-permute-start(f32[64,512]{1,0:T(8,128)S(1)} %add.343), channel_id=1, source_target_pairs={{0,4},{1,5},{2,6},{3,7},{4,0},{5,1},{6,2},{7,3},{8,12},{9,13},{10,... | collective-permute-start | bytes 393224 | tf_op jit(solution)/shard_map/ppermute | solution.py:82
  389.0 5.5 %collective-permute-start.43 = (f32[64,512]{1,0:T(8,128)S(1)}, f32[64,512]{1,0:T(8,128)S(1)}, u32[]{:S(2)}, u32[]{:S(2)}) collective-permute-start(f32[64,512]{1,0:T(8,128)S(1)} %add.349), channel_id=1, source_target_pairs={{0,4},{1,5},{2,6},{3,7},{4,0},{5,1},{6,2},{7,3},{8,12},{9,13},{10,... | collective-permute-start | bytes 393224 | tf_op jit(solution)/shard_map/ppermute | solution.py:82
  389.9 5.6 %collective-permute-start.36 = (f32[128,512]{1,0:T(8,128)S(1)}, f32[128,512]{1,0:T(8,128)S(1)}, u32[]{:S(2)}, u32[]{:S(2)}) collective-permute-start(f32[128,512]{1,0:T(8,128)S(1)} %pad_maximum_fusion.6), channel_id=1, source_target_pairs={{0,2},{1,3},{2,0},{3,1},{4,6},{5,7},{6,4},{7,5},{8,10},{9,11},{10,... | collective-permute-start | bytes 786440 | tf_op jit(solution)/shard_map/ppermute | solution.py:82
  394.5 8.9 %collective-permute-start.44 = (f32[128,512]{1,0:T(8,128)S(1)}, f32[128,512]{1,0:T(8,128)S(1)}, u32[]{:S(2)}, u32[]{:S(2)}) collective-permute-start(f32[128,512]{1,0:T(8,128)S(1)} %pad_maximum_fusion.7), channel_id=1, source_target_pairs={{0,2},{1,3},{2,0},{3,1},{4,6},{5,7},{6,4},{7,5},{8,10},{9,11},{10,... | collective-permute-start | bytes 786440 | tf_op jit(solution)/shard_map/ppermute | solution.py:82
  395.5 12.4 %collective-permute-start.37 = (f32[256,512]{1,0:T(8,128)S(1)}, f32[256,512]{1,0:T(8,128)S(1)}, u32[]{:S(2)}, u32[]{:S(2)}) collective-permute-start(f32[256,512]{1,0:T(8,128)S(1)} %pad_maximum_fusion.4), channel_id=1, source_target_pairs={{0,1},{1,0},{2,3},{3,2},{4,5},{5,4},{6,7},{7,6},{8,9},{9,8},{10,11... | collective-permute-start | bytes 1572872 | tf_op jit(solution)/shard_map/ppermute | solution.py:82
  403.6 4.5 %collective-permute-start.45 = (f32[256,512]{1,0:T(8,128)S(1)}, f32[256,512]{1,0:T(8,128)S(1)}, u32[]{:S(2)}, u32[]{:S(2)}) collective-permute-start(f32[256,512]{1,0:T(8,128)S(1)} %pad_maximum_fusion.5), channel_id=1, source_target_pairs={{0,1},{1,0},{2,3},{3,2},{4,5},{5,4},{6,7},{7,6},{8,9},{9,8},{10,11... | collective-permute-start | bytes 1572872 | tf_op jit(solution)/shard_map/ppermute | solution.py:82
  (23 other events, 329.7 us)

commit v2 on v1

--- a/solution.py
+++ b/solution.py
@@ -83,13 +83,15 @@
 
     def gather_along_rows(own):
         up, down = [own], [own]
-        for _ in range(depth_z - 1):
-            up.append(lax.ppermute(up[-1], "row", [(i, i + 1) for i in range(depth_z - 1)]))
-            down.append(lax.ppermute(down[-1], "row", [(i + 1, i) for i in range(depth_z - 1)]))
+        for step in range(1, depth_z):
+            rising = [(i, i + 1) for i in range(step - 1, depth_z - 1)]
+            falling = [(i + 1, i) for i in range(depth_z - step)]
+            up.append(lax.ppermute(up[-1], "row", rising))
+            down.append(lax.ppermute(down[-1], "row", falling))
         slots = [own]
         for s in range(1, depth_z):
             slots.append(jnp.where(z >= s, up[s], down[depth_z - s]))
-        return jnp.stack(slots)
+        return jnp.stack(slots), (up[depth_z - 2], down[depth_z - 2])
 
     def to_columns(slots):
         got = []
@@ -147,25 +149,37 @@
     keep_blocks, keep_table = rows_of(core)
     send_blocks, send_table = rows_of(1 - core)
 
-    slots = [gather_along_rows(factor[k]) for k in range(2)]
-    pieces = [to_columns(slots[k]) for k in range(2)]
-    panels, diags = [], []
-    for k in range(2):
-        sent = half_product(ancestor, pieces[k], send_table[k], send_blocks, piece_table[k], places)
+    def panel_of(k, pieces):
+        sent = half_product(ancestor, pieces, send_table[k], send_blocks, piece_table[k], places)
         arrived = across(sent, 0)
-        kept = half_product(ancestor, pieces[k], keep_table[k], keep_blocks, piece_table[k], places)
+        kept = half_product(ancestor, pieces, keep_table[k], keep_blocks, piece_table[k], places)
         middle = kept.shape[2] // 2
-        total = kept + arrived
-        left = scatter_rest(total[:, :, :middle], range(1, col_bits))
-        right = scatter_rest(total[:, :, middle:], reversed(range(1, col_bits)))
-        panel = jnp.concatenate([left, right], axis=1)
-        share = lax.dot_general(
+        left = scatter_rest(kept[:, :, :middle] + arrived[:, :, :middle], range(1, col_bits))
+        right = scatter_rest(
+            kept[:, :, middle:] + arrived[:, :, middle:], reversed(range(1, col_bits))
+        )
+        return jnp.concatenate([left, right], axis=1)
+
+    def share_of(k, panel):
+        return lax.dot_general(
             factor[k], panel, (((0,), (0,)), ((), ())),
             precision=lax.Precision.HIGHEST, preferred_element_type=jnp.float32,
         )
-        panels.append(-panel)
-        diags.append(diag_inverse[k] + sum_everywhere(share))
-    return jnp.stack(panels), jnp.stack(diags)
+
+    half = factor.shape[2] // 2
+    gate, panels = None, [[], []]
+    for k in range(2):
+        for start in (0, half):
+            own = factor[k, :, start : start + half]
+            if gate is not None:
+                own, gate = lax.optimization_barrier((own, gate))
+            slots, gate = gather_along_rows(own)
+            panels[k].append(panel_of(k, to_columns(slots)))
+    first = sum_everywhere(share_of(0, jnp.concatenate(panels[0], axis=1)))
+    second = [sum_everywhere(share_of(1, part)) for part in panels[1]]
+    panels = [jnp.concatenate(parts, axis=1) for parts in panels]
+    sums = [first, jnp.concatenate(second, axis=1)]
+    return -jnp.stack(panels), diag_inverse + jnp.stack(sums)
 
 
 def solution(mesh):

time: 412 us -> 418 us (1.015)
  starting transfers between devices: 86.9 us -> 154 us
  waiting for transfers between devices: 225 us -> 159 us
    ppermute x22 -> x38, waiting for transfers between devices: 81.6 us -> 51.4 us  [across(): return lax.ppermute(value, 'col', pairs)]
    ppermute x8 -> x16, waiting for transfers between devices: 48.3 us -> 21.6 us  [to_columns(): got.append(lax.ppermute(value, 'col', pairs))]
    ppermute x8 -> x16, starting transfers between devices: 25.8 us -> 52.4 us  [to_columns(): got.append(lax.ppermute(value, 'col', pairs))]
    ppermute x22 -> x38, starting transfers between devices: 25.3 us -> 48.9 us  [across(): return lax.ppermute(value, 'col', pairs)]
    ppermute x4 -> x6, starting transfers between devices: 0.5 us -> 10.9 us  [sum_everywhere(): value = value + lax.ppermute(value, 'row', pairs)]
    ppermute x12 -> x24, waiting for transfers between devices: 84.9 us -> 76.8 us  [the longest x12 76.8 us: gather_along_rows(): down.append(lax.ppermute(down[-1], 'row', falling))]
    ppermute x12 -> x24, starting transfers between devices: 35.3 us -> 42.2 us  [the longest x12 26.8 us: gather_along_rows(): up.append(lax.ppermute(up[-1], 'row', rising))]
    dynamic_slice x0 -> x8, local copies, waits for them, and re-layouts: none -> 6.32 us  [the longest x6 5.48 us: sum_everywhere(): keep = lax.dynamic_index_in_dim(halves, mine, 0, keepdims=False)]
  transfers between devices with their start and end apart: 46 -> 84, of which waited for: 24 -> 28; matrix products, arithmetic and copies ran while one was open for 9% -> 10% of each run, Pallas kernels for 12% -> 13%
where the time goes in v2:
time: 418 us; the launch traced here: 414 us
  waiting for transfers between devices  159 us (38%)
  starting transfers between devices  154 us (37%)
  Pallas kernels  53 us (13%)
  other arithmetic  24.3 us (6%)
  local copies, waits for them, and re-layouts  16.5 us (4%)
  matrix products  4.79 us (1%)
    ppermute x12, waiting for transfers between devices, gather_along_rows(): down.append(lax.ppermute(down[-1], 'row', falling))  76.8 us
    pallas_call x8, Pallas kernels, half_product(): pl.pallas_call(functools.partial(product_kernel, rows, count), out_shape=...  53 us
    ppermute x16, starting transfers between devices, to_columns(): got.append(lax.ppermute(value, 'col', pairs))  52.4 us
    ppermute x38, waiting for transfers between devices, across(): return lax.ppermute(value, 'col', pairs)  51.4 us
    ppermute x38, starting transfers between devices, across(): return lax.ppermute(value, 'col', pairs)  48.9 us
    ppermute x12, starting transfers between devices, gather_along_rows(): up.append(lax.ppermute(up[-1], 'row', rising))  26.8 us
    ppermute x16, waiting for transfers between devices, to_columns(): got.append(lax.ppermute(value, 'col', pairs))  21.6 us
    ppermute x12, starting transfers between devices, gather_along_rows(): down.append(lax.ppermute(down[-1], 'row', falling))  15.4 us
  transfers between devices with their start and end apart: 84, of which 28 were waited for; matrix products, arithmetic and copies ran while one was open for 10% of the time, Pallas kernels for 13%

profile of v2, /device:TPU:1, one launch (start us, length us, event | category | flops | bytes accessed | tf_op | source)
XLA Modules:
  0.0 413.7 jit_solution(14446165296860554053)
XLA Ops:
  3.7 5.5 %collective-permute-start = (f32[512,256]{1,0:T(8,128)S(1)}, f32[512,256]{1,0:T(8,128)}, u32[]{:S(2)}, u32[]{:S(2)}) collective-permute-start(f32[512,256]{1,0:T(8,128)S(1)} %get-tuple-element.24), channel_id=1, source_target_pairs={{0,8},{8,16},{16,24},{1,9},{9,17},{17,25},{2,10},{10,18},{18,26},{... | collective-permute-start | bytes 1572872 | tf_op jit(solution)/shard_map/ppermute | solution.py:89
  10.1 8.0 %collective-permute-done.1 = f32[512,256]{1,0:T(8,128)S(1)} collective-permute-done((f32[512,256]{1,0:T(8,128)S(1)}, f32[512,256]{1,0:T(8,128)S(1)}, u32[]{:S(2)}, u32[]{:S(2)}) %collective-permute-start.1) | collective-permute-done | bytes 524320 | tf_op jit(solution)/shard_map/ppermute | solution.py:90
  20.1 12.1 %collective-permute-done.2 = f32[512,256]{1,0:T(8,128)} collective-permute-done((f32[512,256]{1,0:T(8,128)S(1)}, f32[512,256]{1,0:T(8,128)}, u32[]{:S(2)}, u32[]{:S(2)}) %collective-permute-start.2) | collective-permute-done | bytes 524320 | tf_op jit(solution)/shard_map/ppermute | solution.py:90
  33.6 6.3 %collective-permute-start.15 = (f32[512,256]{1,0:T(8,128)S(1)}, f32[512,256]{1,0:T(8,128)}, u32[]{:S(2)}, u32[]{:S(2)}) collective-permute-start(f32[512,256]{1,0:T(8,128)S(1)} %get-tuple-element.5), channel_id=1, source_target_pairs={{0,8},{8,16},{16,24},{1,9},{9,17},{17,25},{2,10},{10,18},{18,26},{... | collective-permute-start | bytes 1572872 | tf_op jit(solution)/shard_map/ppermute | solution.py:89
  43.3 3.5 collective-permute-done.16
  48.8 9.2 %collective-permute-done.3 = f32[512,256]{1,0:T(8,128)} collective-permute-done((f32[512,256]{1,0:T(8,128)}, f32[512,256]{1,0:T(8,128)}, u32[]{:S(2)}, u32[]{:S(2)}) %collective-permute-start.3) | collective-permute-done | bytes 524320 | tf_op jit(solution)/shard_map/ppermute | solution.py:90
  60.2 9.2 %collective-permute-start.6 = (f32[512,256]{1,0:T(8,128)S(1)}, f32[512,256]{1,0:T(8,128)S(1)}, u32[]{:S(2)}, u32[]{:S(2)}) collective-permute-start(f32[512,256]{1,0:T(8,128)S(1)} %get-tuple-element.22), channel_id=1, source_target_pairs={{0,0},{4,1},{1,2},{5,3},{2,4},{6,5},{3,6},{7,7},{8,8},{12,9},{9,10... | collective-permute-start | bytes 1572872 | tf_op jit(solution)/shard_map/ppermute | solution.py:104
  74.1 5.3 %collective-permute-start.30 = (f32[512,256]{1,0:T(8,128)S(1)}, f32[512,256]{1,0:T(8,128)S(1)}, u32[]{:S(2)}, u32[]{:S(2)}) collective-permute-start(f32[512,256]{1,0:T(8,128)S(1)} %get-tuple-element.6), channel_id=1, source_target_pairs={{0,8},{8,16},{16,24},{1,9},{9,17},{17,25},{2,10},{10,18},{18,26},{... | collective-permute-start | bytes 1572872 | tf_op jit(solution)/shard_map/ppermute | solution.py:89
  80.5 3.0 collective-permute-start.8
  83.5 14.6 %collective-permute-done.18 = f32[512,256]{1,0:T(8,128)S(1)} collective-permute-done((f32[512,256]{1,0:T(8,128)S(1)}, f32[512,256]{1,0:T(8,128)S(1)}, u32[]{:S(2)}, u32[]{:S(2)}) %collective-permute-start.18) | collective-permute-done | bytes 524320 | tf_op jit(solution)/shard_map/ppermute | solution.py:90
  98.1 5.2 %collective-permute-start.9 = (f32[512,256]{1,0:T(8,128)S(1)}, f32[512,256]{1,0:T(8,128)S(1)}, u32[]{:S(2)}, u32[]{:S(2)}) collective-permute-start(f32[512,256]{1,0:T(8,128)S(1)} %get-tuple-element.19), channel_id=1, source_target_pairs={{3,0},{7,1},{0,2},{4,3},{1,4},{5,5},{2,6},{6,7},{11,8},{15,9},{8,1... | collective-permute-start | bytes 1572872 | tf_op jit(solution)/shard_map/ppermute | solution.py:104
  109.6 3.3 collective-permute-start.23
  113.0 5.6 %collective-permute-done.32 = f32[512,256]{1,0:T(8,128)S(1)} collective-permute-done((f32[512,256]{1,0:T(8,128)S(1)}, f32[512,256]{1,0:T(8,128)S(1)}, u32[]{:S(2)}, u32[]{:S(2)}) %collective-permute-start.32) | collective-permute-done | bytes 524320 | tf_op jit(solution)/shard_map/ppermute | solution.py:90
  120.5 7.9 %shard_map.60 = f32[4,512,256]{2,1,0:T(8,128)S(1)} custom-call(s32[16]{0:T(128)S(1)} %get-tuple-element.67.meta, f32[4096,2048]{1,0:T(8,128)} %a_ref.15, f32[512,256]{1,0:T(8,128)S(1)} %collective-permute-done.6.refs_0_, f32[512,256]{1,0:T(8,128)S(1)} %collective-permute-done.7.refs_1_, f32[512,256]{1,0:T(8,128)S(1)} %collective-permute-done.8.refs_2_, ...), custom_call_target="tpu_custom_call" | custom-call | flops 3221225472 | bytes 8388608 | tf_op jit(solution)/shard_map/pallas_call | solution.py:52
  128.5 6.7 %shard_map.59 = f32[4,512,256]{2,1,0:T(8,128)S(1)} custom-call(s32[16]{0:T(128)S(1)} %get-tuple-element.66.meta, f32[4096,2048]{1,0:T(8,128)} %a_ref.15, f32[512,256]{1,0:T(8,128)S(1)} %collective-permute-done.6.refs_0_, f32[512,256]{1,0:T(8,128)S(1)} %collective-permute-done.7.refs_1_, f32[512,256]{1,0:T(8,128)S(1)} %collective-permute-done.8.refs_2_, ...), custom_call_target="tpu_custom_call" | custom-call | flops 3221225472 | bytes 8388608 | tf_op jit(solution)/shard_map/pallas_call | solution.py:52
  136.5 4.0 collective-permute-start.45
  142.6 6.7 %shard_map.61 = f32[4,512,256]{2,1,0:T(8,128)S(1)} custom-call(s32[16]{0:T(128)S(1)} %get-tuple-element.66.meta, f32[4096,2048]{1,0:T(8,128)} %a_ref.15, f32[512,256]{1,0:T(8,128)S(1)} %collective-permute-done.21.refs_0_, f32[512,256]{1,0:T(8,128)S(1)} %collective-permute-done.22.refs_1_, f32[512,256]{1,0:T(8,128)S(1)} %collective-permute-done.23.refs_2_, ...), custom_call_target="tpu_custom_call" | custom-call | flops 3221225472 | bytes 8388608 | tf_op jit(solution)/shard_map/pallas_call | solution.py:52
  149.2 7.9 %shard_map.62 = f32[4,512,256]{2,1,0:T(8,128)S(1)} custom-call(s32[16]{0:T(128)S(1)} %get-tuple-element.67.meta, f32[4096,2048]{1,0:T(8,128)} %a_ref.15, f32[512,256]{1,0:T(8,128)S(1)} %collective-permute-done.21.refs_0_, f32[512,256]{1,0:T(8,128)S(1)} %collective-permute-done.22.refs_1_, f32[512,256]{1,0:T(8,128)S(1)} %collective-permute-done.23.refs_2_, ...), custom_call_target="tpu_custom_call" | custom-call | flops 3221225472 | bytes 8388608 | tf_op jit(solution)/shard_map/pallas_call | solution.py:52
  157.3 4.0 collective-permute-done.33
  161.7 5.5 %collective-permute-start.36 = (f32[512,256]{1,0:T(8,128)S(1)}, f32[512,256]{1,0:T(8,128)S(1)}, u32[]{:S(2)}, u32[]{:S(2)}) collective-permute-start(f32[512,256]{1,0:T(8,128)S(1)} %get-tuple-element.35), channel_id=1, source_target_pairs={{0,0},{4,1},{1,2},{5,3},{2,4},{6,5},{3,6},{7,7},{8,8},{12,9},{9,10... | collective-permute-start | bytes 1572872 | tf_op jit(solution)/shard_map/ppermute | solution.py:104
  174.0 2.4 collective-permute-done.36.refs_0_
  179.2 10.2 %collective-permute-done.38.refs_2_ = f32[512,256]{1,0:T(8,128)S(1)} collective-permute-done((f32[512,256]{1,0:T(8,128)S(1)}, f32[512,256]{1,0:T(8,128)S(1)}, u32[]{:S(2)}, u32[]{:S(2)}) %collective-permute-start.38) | collective-permute-done | bytes 524320 | tf_op jit(solution)/shard_map/ppermute | solution.py:104
  189.4 3.2 collective-permute-start.11
  192.7 6.3 %shard_map.63 = f32[4,512,256]{2,1,0:T(8,128)S(1)} custom-call(s32[16]{0:T(128)S(1)} %get-tuple-element.78.meta, f32[4096,2048]{1,0:T(8,128)} %a_ref.15, f32[512,256]{1,0:T(8,128)S(1)} %collective-permute-done.36.refs_0_, f32[512,256]{1,0:T(8,128)S(1)} %collective-permute-done.37.refs_1_, f32[512,256]{1,0:T(8,128)S(1)} %collective-permute-done.38.refs_2_, ...), custom_call_target="tpu_custom_call" | custom-call | flops 3221225472 | bytes 8388608 | tf_op jit(solution)/shard_map/pallas_call | solution.py:52
  199.0 4.8 %shard_map.64 = f32[4,512,256]{2,1,0:T(8,128)S(1)} custom-call(s32[16]{0:T(128)S(1)} %get-tuple-element.79.meta, f32[4096,2048]{1,0:T(8,128)} %a_ref.15, f32[512,256]{1,0:T(8,128)S(1)} %collective-permute-done.36.refs_0_, f32[512,256]{1,0:T(8,128)S(1)} %collective-permute-done.37.refs_1_, f32[512,256]{1,0:T(8,128)S(1)} %collective-permute-done.38.refs_2_, ...), custom_call_target="tpu_custom_call" | custom-call | flops 3221225472 | bytes 8388608 | tf_op jit(solution)/shard_map/pallas_call | solution.py:52
  208.9 19.8 %collective-permute-done.48 = f32[512,256]{1,0:T(8,128)S(1)} collective-permute-done((f32[512,256]{1,0:T(8,128)S(1)}, f32[512,256]{1,0:T(8,128)S(1)}, u32[]{:S(2)}, u32[]{:S(2)}) %collective-permute-start.48) | collective-permute-done | bytes 524320 | tf_op jit(solution)/shard_map/ppermute | solution.py:90
  231.7 4.4 %collective-permute-start.51 = (f32[512,256]{1,0:T(8,128)S(1)}, f32[512,256]{1,0:T(8,128)S(1)}, u32[]{:S(2)}, u32[]{:S(2)}) collective-permute-start(f32[512,256]{1,0:T(8,128)S(1)} %get-tuple-element.39), channel_id=1, source_target_pairs={{0,0},{4,1},{1,2},{5,3},{2,4},{6,5},{3,6},{7,7},{8,8},{12,9},{9,10... | collective-permute-start | bytes 1572872 | tf_op jit(solution)/shard_map/ppermute | solution.py:104
  236.4 11.8 %collective-permute-done.26 = f32[2,512,128]{2,1,0:T(8,128)S(1)} collective-permute-done((f32[2,512,128]{2,1,0:T(8,128)S(1)}, f32[2,512,128]{2,1,0:T(8,128)S(1)}, u32[]{:S(2)}, u32[]{:S(2)}) %collective-permute-start.26) | collective-permute-done | bytes 524320 | tf_op jit(solution)/shard_map/ppermute | solution.py:82
  248.2 3.4 collective-permute-start.52
  251.9 2.6 collective-permute-start.29
  254.6 10.2 %collective-permute-done.27 = f32[1,512,128]{2,1,0:T(8,128)S(1)} collective-permute-done((f32[1,512,128]{2,1,0:T(8,128)S(1)}, f32[1,512,128]{2,1,0:T(8,128)S(1)}, u32[]{:S(2)}, u32[]{:S(2)}) %collective-permute-start.27) | collective-permute-done | bytes 262176 | tf_op jit(solution)/shard_map/ppermute | solution.py:82
  264.7 3.1 collective-permute-start.53
  272.0 5.2 %collective-permute-done.53.refs_2_ = f32[512,256]{1,0:T(8,128)S(1)} collective-permute-done((f32[512,256]{1,0:T(8,128)S(1)}, f32[512,256]{1,0:T(8,128)S(1)}, u32[]{:S(2)}, u32[]{:S(2)}) %collective-permute-start.53) | collective-permute-done | bytes 524320 | tf_op jit(solution)/shard_map/ppermute | solution.py:104
  277.2 3.1 collective-permute-done.54.refs_3_
  280.3 6.3 %shard_map.66 = f32[4,512,256]{2,1,0:T(8,128)} custom-call(s32[16]{0:T(128)S(1)} %get-tuple-element.79.meta, f32[4096,2048]{1,0:T(8,128)} %a_ref.15, f32[512,256]{1,0:T(8,128)S(1)} %collective-permute-done.51.refs_0_, f32[512,256]{1,0:T(8,128)S(1)} %collective-permute-done.52.refs_1_, f32[512,256]{1,0:T(8,128)S(1)} %collective-permute-done.53.refs_2_, ...), custom_call_target="tpu_custom_call" | custom-call | flops 3221225472 | bytes 8388608 | tf_op jit(solution)/shard_map/pallas_call | solution.py:52
  288.2 2.9 collective-permute-start.41
  291.3 6.5 %shard_map.65 = f32[4,512,256]{2,1,0:T(8,128)S(1)} custom-call(s32[16]{0:T(128)S(1)} %get-tuple-element.78.meta, f32[4096,2048]{1,0:T(8,128)} %a_ref.15, f32[512,256]{1,0:T(8,128)S(1)} %collective-permute-done.51.refs_0_, f32[512,256]{1,0:T(8,128)S(1)} %collective-permute-done.52.refs_1_, f32[512,256]{1,0:T(8,128)S(1)} %collective-permute-done.53.refs_2_, ...), custom_call_target="tpu_custom_call" | custom-call | flops 3221225472 | bytes 8388608 | tf_op jit(solution)/shard_map/pallas_call | solution.py:52
  298.8 10.2 %collective-permute-done.61 = f32[128,512]{1,0:T(8,128)S(1)} collective-permute-done((f32[128,512]{1,0:T(8,128)S(1)}, f32[128,512]{1,0:T(8,128)S(1)}, u32[]{:S(2)}, u32[]{:S(2)}) %collective-permute-start.61) | collective-permute-done | bytes 262176 | tf_op jit(solution)/shard_map/ppermute | solution.py:82
  313.9 6.0 %collective-permute-start.63 = (f32[64,512]{1,0:T(8,128)S(1)}, f32[64,512]{1,0:T(8,128)S(1)}, u32[]{:S(2)}, u32[]{:S(2)}) collective-permute-start(f32[64,512]{1,0:T(8,128)S(1)} %bitcast_add_fusion.14), channel_id=1, source_target_pairs={{0,8},{8,0},{16,24},{24,16},{1,9},{9,1},{17,25},{25,17},{2,10},{10... | collective-permute-start | bytes 393224 | tf_op jit(solution)/shard_map/ppermute | solution.py:132
  320.0 2.7 collective-permute-done.63
  329.5 2.5 collective-permute-done.64
  333.6 3.1 slice_add_fusion.1
  349.9 9.2 %collective-permute-done.70 = f32[64,256]{1,0:T(8,128)S(1)} collective-permute-done((f32[64,256]{1,0:T(8,128)S(1)}, f32[64,256]{1,0:T(8,128)S(1)}, u32[]{:S(2)}, u32[]{:S(2)}) %collective-permute-start.70) | collective-permute-done | bytes 65568 | tf_op jit(solution)/shard_map/ppermute | solution.py:82
  366.8 2.4 collective-permute-done.59
  371.2 5.4 %collective-permute-start.76 = (f32[256,256]{0,1:T(8,128)S(1)}, f32[256,256]{0,1:T(8,128)S(1)}, u32[]{:S(2)}, u32[]{:S(2)}) collective-permute-start(f32[256,256]{0,1:T(8,128)S(1)} %bitcast.251), channel_id=1, source_target_pairs={{0,1},{1,0},{2,3},{3,2},{4,5},{5,4},{6,7},{7,6},{8,9},{9,8},{10,11... | collective-permute-start | bytes 786440 | tf_op jit(solution)/shard_map/ppermute | solution.py:82
  390.7 2.3 collective-permute-start.75
  394.3 3.5 collective-permute-done.80
  405.0 5.3 %collective-permute-start.83 = (f32[256,256]{1,0:T(8,128)S(1)}, f32[256,256]{1,0:T(8,128)S(1)}, u32[]{:S(2)}, u32[]{:S(2)}) collective-permute-start(f32[256,256]{1,0:T(8,128)S(1)} %pad_maximum_fusion.9), channel_id=1, source_target_pairs={{0,1},{1,0},{2,3},{3,2},{4,5},{5,4},{6,7},{7,6},{8,9},{9,8},{10,11... | collective-permute-start | bytes 786440 | tf_op jit(solution)/shard_map/ppermute | solution.py:82
  (286 shorter events, 119.6 us)
Async XLA Ops:
  2.4 15.7 %collective-permute-start.1 = (f32[512,256]{1,0:T(8,128)S(1)}, f32[512,256]{1,0:T(8,128)S(1)}, u32[]{:S(2)}, u32[]{:S(2)}) collective-permute-start(f32[512,256]{1,0:T(8,128)S(1)} %get-tuple-element.24), channel_id=1, source_target_pairs={{8,0},{16,8},{24,16},{9,1},{17,9},{25,17},{10,2},{18,10},{26,18},{... | collective-permute-start | bytes 1572872 | tf_op jit(solution)/shard_map/ppermute | solution.py:90
  3.7 15.7 %collective-permute-start = (f32[512,256]{1,0:T(8,128)S(1)}, f32[512,256]{1,0:T(8,128)}, u32[]{:S(2)}, u32[]{:S(2)}) collective-permute-start(f32[512,256]{1,0:T(8,128)S(1)} %get-tuple-element.24), channel_id=1, source_target_pairs={{0,8},{8,16},{16,24},{1,9},{9,17},{17,25},{2,10},{10,18},{18,26},{... | collective-permute-start | bytes 1572872 | tf_op jit(solution)/shard_map/ppermute | solution.py:89
  39.8 18.2 %collective-permute-start.3 = (f32[512,256]{1,0:T(8,128)}, f32[512,256]{1,0:T(8,128)}, u32[]{:S(2)}, u32[]{:S(2)}) collective-permute-start(f32[512,256]{1,0:T(8,128)} %collective-permute-done.2), channel_id=1, source_target_pairs={{8,0},{9,1},{10,2},{11,3},{12,4},{13,5},{14,6},{15,7}} | collective-permute-start | bytes 1572872 | tf_op jit(solution)/shard_map/ppermute | solution.py:90
  41.5 17.6 %collective-permute-start.5 = (f32[512,256]{1,0:T(8,128)}, f32[512,256]{1,0:T(8,128)S(1)}, u32[]{:S(2)}, u32[]{:S(2)}) collective-permute-start(f32[512,256]{1,0:T(8,128)} %copy-done.9), channel_id=1, source_target_pairs={{16,24},{17,25},{18,26},{19,27},{20,28},{21,29},{22,30},{23,31}} | collective-permute-start | bytes 1572872 | tf_op jit(solution)/shard_map/ppermute | solution.py:89
  46.8 24.6 %collective-permute-start.17 = (f32[512,256]{1,0:T(8,128)}, f32[512,256]{1,0:T(8,128)S(1)}, u32[]{:S(2)}, u32[]{:S(2)}) collective-permute-start(f32[512,256]{1,0:T(8,128)} %collective-permute-done.16), channel_id=1, source_target_pairs={{8,0},{16,8},{9,1},{17,9},{10,2},{18,10},{11,3},{19,11},{12,4},{20... | collective-permute-start | bytes 1572872 | tf_op jit(solution)/shard_map/ppermute | solution.py:90
  60.2 20.2 %collective-permute-start.6 = (f32[512,256]{1,0:T(8,128)S(1)}, f32[512,256]{1,0:T(8,128)S(1)}, u32[]{:S(2)}, u32[]{:S(2)}) collective-permute-start(f32[512,256]{1,0:T(8,128)S(1)} %get-tuple-element.22), channel_id=1, source_target_pairs={{0,0},{4,1},{1,2},{5,3},{2,4},{6,5},{3,6},{7,7},{8,8},{12,9},{9,10... | collective-permute-start | bytes 1572872 | tf_op jit(solution)/shard_map/ppermute | solution.py:104
  69.4 36.3 %collective-permute-start.7 = (f32[512,256]{1,0:T(8,128)S(1)}, f32[512,256]{1,0:T(8,128)S(1)}, u32[]{:S(2)}, u32[]{:S(2)}) collective-permute-start(f32[512,256]{1,0:T(8,128)S(1)} %get-tuple-element.21), channel_id=1, source_target_pairs={{1,0},{5,1},{2,2},{6,3},{3,4},{7,5},{0,6},{4,7},{9,8},{13,9},{10,1... | collective-permute-start | bytes 1572872 | tf_op jit(solution)/shard_map/ppermute | solution.py:104
  71.4 32.0 %collective-permute-start.31 = (f32[512,256]{1,0:T(8,128)S(1)}, f32[512,256]{1,0:T(8,128)S(1)}, u32[]{:S(2)}, u32[]{:S(2)}) collective-permute-start(f32[512,256]{1,0:T(8,128)S(1)} %get-tuple-element.6), channel_id=1, source_target_pairs={{8,0},{16,8},{24,16},{9,1},{17,9},{25,17},{10,2},{18,10},{26,18},{... | collective-permute-start | bytes 1572872 | tf_op jit(solution)/shard_map/ppermute | solution.py:90
  72.7 25.4 %collective-permute-start.18 = (f32[512,256]{1,0:T(8,128)S(1)}, f32[512,256]{1,0:T(8,128)S(1)}, u32[]{:S(2)}, u32[]{:S(2)}) collective-permute-start(f32[512,256]{1,0:T(8,128)S(1)} %collective-permute-done.17), channel_id=1, source_target_pairs={{8,0},{9,1},{10,2},{11,3},{12,4},{13,5},{14,6},{15,7}} | collective-permute-start | bytes 1572872 | tf_op jit(solution)/shard_map/ppermute | solution.py:90
  74.1 30.7 %collective-permute-start.30 = (f32[512,256]{1,0:T(8,128)S(1)}, f32[512,256]{1,0:T(8,128)S(1)}, u32[]{:S(2)}, u32[]{:S(2)}) collective-permute-start(f32[512,256]{1,0:T(8,128)S(1)} %get-tuple-element.6), channel_id=1, source_target_pairs={{0,8},{8,16},{16,24},{1,9},{9,17},{17,25},{2,10},{10,18},{18,26},{... | collective-permute-start | bytes 1572872 | tf_op jit(solution)/shard_map/ppermute | solution.py:89
  80.5 27.2 %collective-permute-start.8 = (f32[512,256]{1,0:T(8,128)S(1)}, f32[512,256]{1,0:T(8,128)S(1)}, u32[]{:S(2)}, u32[]{:S(2)}) collective-permute-start(f32[512,256]{1,0:T(8,128)S(1)} %get-tuple-element.20), channel_id=1, source_target_pairs={{2,0},{6,1},{3,2},{7,3},{0,4},{4,5},{1,6},{5,7},{10,8},{14,9},{11,... | collective-permute-start | bytes 1572872 | tf_op jit(solution)/shard_map/ppermute | solution.py:104
  103.3 15.3 %collective-permute-start.32 = (f32[512,256]{1,0:T(8,128)S(1)}, f32[512,256]{1,0:T(8,128)S(1)}, u32[]{:S(2)}, u32[]{:S(2)}) collective-permute-start(f32[512,256]{1,0:T(8,128)S(1)} %collective-permute-done.31), channel_id=1, source_target_pairs={{8,0},{16,8},{9,1},{17,9},{10,2},{18,10},{11,3},{19,11},{12,4},{20... | collective-permute-start | bytes 1572872 | tf_op jit(solution)/shard_map/ppermute | solution.py:90
  104.7 23.6 %collective-permute-start.34 = (f32[512,256]{1,0:T(8,128)S(1)}, f32[512,256]{1,0:T(8,128)S(1)}, u32[]{:S(2)}, u32[]{:S(2)}) collective-permute-start(f32[512,256]{1,0:T(8,128)S(1)} %collective-permute-done.30), channel_id=1, source_target_pairs={{8,16},{16,24},{9,17},{17,25},{10,18},{18,26},{11,19},{19,27},{12,... | collective-permute-start | bytes 1572872 | tf_op jit(solution)/shard_map/ppermute | solution.py:89
  105.8 29.4 %collective-permute-start.21 = (f32[512,256]{1,0:T(8,128)S(1)}, f32[512,256]{1,0:T(8,128)S(1)}, u32[]{:S(2)}, u32[]{:S(2)}) collective-permute-start(f32[512,256]{1,0:T(8,128)S(1)} %get-tuple-element.31), channel_id=1, source_target_pairs={{0,0},{4,1},{1,2},{5,3},{2,4},{6,5},{3,6},{7,7},{8,8},{12,9},{9,10... | collective-permute-start | bytes 1572872 | tf_op jit(solution)/shard_map/ppermute | solution.py:104
  107.7 28.8 %collective-permute-start.22 = (f32[512,256]{1,0:T(8,128)S(1)}, f32[512,256]{1,0:T(8,128)S(1)}, u32[]{:S(2)}, u32[]{:S(2)}) collective-permute-start(f32[512,256]{1,0:T(8,128)S(1)} %get-tuple-element.30), channel_id=1, source_target_pairs={{1,0},{5,1},{2,2},{6,3},{3,4},{7,5},{0,6},{4,7},{9,8},{13,9},{10,1... | collective-permute-start | bytes 1572872 | tf_op jit(solution)/shard_map/ppermute | solution.py:104
  109.6 30.9 %collective-permute-start.23 = (f32[512,256]{1,0:T(8,128)S(1)}, f32[512,256]{1,0:T(8,128)S(1)}, u32[]{:S(2)}, u32[]{:S(2)}) collective-permute-start(f32[512,256]{1,0:T(8,128)S(1)} %get-tuple-element.29), channel_id=1, source_target_pairs={{2,0},{6,1},{3,2},{7,3},{0,4},{4,5},{1,6},{5,7},{10,8},{14,9},{11,... | collective-permute-start | bytes 1572872 | tf_op jit(solution)/shard_map/ppermute | solution.py:104
  118.6 22.7 %collective-permute-start.24 = (f32[512,256]{1,0:T(8,128)S(1)}, f32[512,256]{1,0:T(8,128)S(1)}, u32[]{:S(2)}, u32[]{:S(2)}) collective-permute-start(f32[512,256]{1,0:T(8,128)S(1)} %get-tuple-element.28), channel_id=1, source_target_pairs={{3,0},{7,1},{0,2},{4,3},{1,4},{5,5},{2,6},{6,7},{11,8},{15,9},{8,1... | collective-permute-start | bytes 1572872 | tf_op jit(solution)/shard_map/ppermute | solution.py:104
  128.4 42.6 %collective-permute-start.10 = (f32[4,512,256]{2,1,0:T(8,128)S(1)}, f32[4,512,256]{2,1,0:T(8,128)S(1)}, u32[]{:S(2)}, u32[]{:S(2)}) collective-permute-start(f32[4,512,256]{2,1,0:T(8,128)S(1)} %shard_map.60), channel_id=1, source_target_pairs={{0,1},{1,0},{2,3},{3,2},{4,5},{5,4},{6,7},{7,6},{8,9},{9,8},{10,11... | collective-permute-start | bytes 6291464 | tf_op jit(solution)/shard_map/ppermute | solution.py:82
  135.2 33.9 %collective-permute-start.46 = (f32[512,256]{1,0:T(8,128)S(1)}, f32[512,256]{1,0:T(8,128)S(1)}, u32[]{:S(2)}, u32[]{:S(2)}) collective-permute-start(f32[512,256]{1,0:T(8,128)S(1)} %get-tuple-element.7), channel_id=1, source_target_pairs={{8,0},{16,8},{24,16},{9,1},{17,9},{25,17},{10,2},{18,10},{26,18},{... | collective-permute-start | bytes 1572872 | tf_op jit(solution)/shard_map/ppermute | solution.py:90
  136.5 36.8 %collective-permute-start.45 = (f32[512,256]{1,0:T(8,128)S(1)}, f32[512,256]{1,0:T(8,128)S(1)}, u32[]{:S(2)}, u32[]{:S(2)}) collective-permute-start(f32[512,256]{1,0:T(8,128)S(1)} %get-tuple-element.7), channel_id=1, source_target_pairs={{0,8},{8,16},{16,24},{1,9},{9,17},{17,25},{2,10},{10,18},{18,26},{... | collective-permute-start | bytes 1572872 | tf_op jit(solution)/shard_map/ppermute | solution.py:89
  140.6 16.6 %collective-permute-start.35 = (f32[512,256]{1,0:T(8,128)S(1)}, f32[512,256]{1,0:T(8,128)S(1)}, u32[]{:S(2)}, u32[]{:S(2)}) collective-permute-start(f32[512,256]{1,0:T(8,128)S(1)} %collective-permute-done.34), channel_id=1, source_target_pairs={{16,24},{17,25},{18,26},{19,27},{20,28},{21,29},{22,30},{23,31}} | collective-permute-start | bytes 1572872 | tf_op jit(solution)/shard_map/ppermute | solution.py:89
  141.3 20.0 %collective-permute-start.33 = (f32[512,256]{1,0:T(8,128)S(1)}, f32[512,256]{1,0:T(8,128)S(1)}, u32[]{:S(2)}, u32[]{:S(2)}) collective-permute-start(f32[512,256]{1,0:T(8,128)S(1)} %collective-permute-done.32), channel_id=1, source_target_pairs={{8,0},{9,1},{10,2},{11,3},{12,4},{13,5},{14,6},{15,7}} | collective-permute-start | bytes 1572872 | tf_op jit(solution)/shard_map/ppermute | solution.py:90
  169.1 20.3 %collective-permute-start.38 = (f32[512,256]{1,0:T(8,128)S(1)}, f32[512,256]{1,0:T(8,128)S(1)}, u32[]{:S(2)}, u32[]{:S(2)}) collective-permute-start(f32[512,256]{1,0:T(8,128)S(1)} %get-tuple-element.33), channel_id=1, source_target_pairs={{2,0},{6,1},{3,2},{7,3},{0,4},{4,5},{1,6},{5,7},{10,8},{14,9},{11,... | collective-permute-start | bytes 1572872 | tf_op jit(solution)/shard_map/ppermute | solution.py:104
  171.0 21.7 %collective-permute-start.39 = (f32[512,256]{1,0:T(8,128)S(1)}, f32[512,256]{1,0:T(8,128)S(1)}, u32[]{:S(2)}, u32[]{:S(2)}) collective-permute-start(f32[512,256]{1,0:T(8,128)S(1)} %get-tuple-element.32), channel_id=1, source_target_pairs={{3,0},{7,1},{0,2},{4,3},{1,4},{5,5},{2,6},{6,7},{11,8},{15,9},{8,1... | collective-permute-start | bytes 1572872 | tf_op jit(solution)/shard_map/ppermute | solution.py:104
  173.3 57.9 %collective-permute-start.25 = (f32[4,512,256]{2,1,0:T(8,128)S(1)}, f32[4,512,256]{2,1,0:T(8,128)S(1)}, u32[]{:S(2)}, u32[]{:S(2)}) collective-permute-start(f32[4,512,256]{2,1,0:T(8,128)S(1)} %shard_map.62), channel_id=1, source_target_pairs={{0,1},{1,0},{2,3},{3,2},{4,5},{5,4},{6,7},{7,6},{8,9},{9,8},{10,11... | collective-permute-start | bytes 6291464 | tf_op jit(solution)/shard_map/ppermute | solution.py:82
  176.3 27.5 %collective-permute-start.47 = (f32[512,256]{1,0:T(8,128)S(1)}, f32[512,256]{1,0:T(8,128)S(1)}, u32[]{:S(2)}, u32[]{:S(2)}) collective-permute-start(f32[512,256]{1,0:T(8,128)S(1)} %collective-permute-done.46), channel_id=1, source_target_pairs={{8,0},{16,8},{9,1},{17,9},{10,2},{18,10},{11,3},{19,11},{12,4},{20... | collective-permute-start | bytes 1572872 | tf_op jit(solution)/shard_map/ppermute | solution.py:90
  178.3 27.1 %collective-permute-start.49 = (f32[512,256]{1,0:T(8,128)S(1)}, f32[512,256]{1,0:T(8,128)S(1)}, u32[]{:S(2)}, u32[]{:S(2)}) collective-permute-start(f32[512,256]{1,0:T(8,128)S(1)} %collective-permute-done.45), channel_id=1, source_target_pairs={{8,16},{16,24},{9,17},{17,25},{10,18},{18,26},{11,19},{19,27},{12,... | collective-permute-start | bytes 1572872 | tf_op jit(solution)/shard_map/ppermute | solution.py:89
  189.4 17.3 %collective-permute-start.11 = (f32[2,512,128]{2,1,0:T(8,128)S(1)}, f32[2,512,128]{2,1,0:T(8,128)S(1)}, u32[]{:S(2)}, u32[]{:S(2)}) collective-permute-start(f32[2,512,128]{2,1,0:T(8,128)S(1)} %dynamic-slice_bitcast_fusion.20), channel_id=1, source_target_pairs={{0,2},{1,3},{2,0},{3,1},{4,6},{5,7},{6,4},{7,5},{8,10},{9,11},{10,... | collective-permute-start | bytes 1572872 | tf_op jit(solution)/shard_map/ppermute | solution.py:82
  192.7 14.9 %collective-permute-start.13 = (f32[2,512,128]{2,1,0:T(8,128)S(1)}, f32[2,512,128]{2,1,0:T(8,128)S(1)}, u32[]{:S(2)}, u32[]{:S(2)}) collective-permute-start(f32[2,512,128]{2,1,0:T(8,128)S(1)} %dynamic-slice_bitcast_fusion.19), channel_id=1, source_target_pairs={{0,4},{1,5},{2,6},{3,7},{4,0},{5,1},{6,2},{7,3},{8,12},{9,13},{10,... | collective-permute-start | bytes 1572872 | tf_op jit(solution)/shard_map/ppermute | solution.py:82
  203.8 84.2 %collective-permute-start.40 = (f32[4,512,256]{2,1,0:T(8,128)S(1)}, f32[4,512,256]{2,1,0:T(8,128)S(1)}, u32[]{:S(2)}, u32[]{:S(2)}) collective-permute-start(f32[4,512,256]{2,1,0:T(8,128)S(1)} %shard_map.64), channel_id=1, source_target_pairs={{0,1},{1,0},{2,3},{3,2},{4,5},{5,4},{6,7},{7,6},{8,9},{9,8},{10,11... | collective-permute-start | bytes 6291464 | tf_op jit(solution)/shard_map/ppermute | solution.py:82
  205.4 23.2 %collective-permute-start.48 = (f32[512,256]{1,0:T(8,128)S(1)}, f32[512,256]{1,0:T(8,128)S(1)}, u32[]{:S(2)}, u32[]{:S(2)}) collective-permute-start(f32[512,256]{1,0:T(8,128)S(1)} %collective-permute-done.47), channel_id=1, source_target_pairs={{8,0},{9,1},{10,2},{11,3},{12,4},{13,5},{14,6},{15,7}} | collective-permute-start | bytes 1572872 | tf_op jit(solution)/shard_map/ppermute | solution.py:90
  206.8 24.2 %collective-permute-start.50 = (f32[512,256]{1,0:T(8,128)S(1)}, f32[512,256]{1,0:T(8,128)S(1)}, u32[]{:S(2)}, u32[]{:S(2)}) collective-permute-start(f32[512,256]{1,0:T(8,128)S(1)} %collective-permute-done.49), channel_id=1, source_target_pairs={{16,24},{17,25},{18,26},{19,27},{20,28},{21,29},{22,30},{23,31}} | collective-permute-start | bytes 1572872 | tf_op jit(solution)/shard_map/ppermute | solution.py:89
  207.6 28.6 %collective-permute-start.12 = (f32[1,512,128]{2,1,0:T(8,128)S(1)}, f32[1,512,128]{2,1,0:T(8,128)S(1)}, u32[]{:S(2)}, u32[]{:S(2)}) collective-permute-start(f32[1,512,128]{2,1,0:T(8,128)S(1)} %constant_dynamic-slice_fusion.15), channel_id=1, source_target_pairs={{0,4},{1,5},{2,6},{3,7},{4,0},{5,1},{6,2},{7,3},{8,12},{9,13},{10,... | collective-permute-start | bytes 786440 | tf_op jit(solution)/shard_map/ppermute | solution.py:82
  228.7 23.3 %collective-permute-start.14 = (f32[1,512,128]{2,1,0:T(8,128)S(1)}, f32[1,512,128]{2,1,0:T(8,128)S(1)}, u32[]{:S(2)}, u32[]{:S(2)}) collective-permute-start(f32[1,512,128]{2,1,0:T(8,128)S(1)} %constant_dynamic-slice_fusion.14), channel_id=1, source_target_pairs={{0,2},{1,3},{2,0},{3,1},{4,6},{5,7},{6,4},{7,5},{8,10},{9,11},{10,... | collective-permute-start | bytes 786440 | tf_op jit(solution)/shard_map/ppermute | solution.py:82
  231.5 16.7 %collective-permute-start.26 = (f32[2,512,128]{2,1,0:T(8,128)S(1)}, f32[2,512,128]{2,1,0:T(8,128)S(1)}, u32[]{:S(2)}, u32[]{:S(2)}) collective-permute-start(f32[2,512,128]{2,1,0:T(8,128)S(1)} %dynamic-slice_bitcast_fusion.14), channel_id=1, source_target_pairs={{0,2},{1,3},{2,0},{3,1},{4,6},{5,7},{6,4},{7,5},{8,10},{9,11},{10,... | collective-permute-start | bytes 1572872 | tf_op jit(solution)/shard_map/ppermute | solution.py:82
  231.7 40.0 %collective-permute-start.51 = (f32[512,256]{1,0:T(8,128)S(1)}, f32[512,256]{1,0:T(8,128)S(1)}, u32[]{:S(2)}, u32[]{:S(2)}) collective-permute-start(f32[512,256]{1,0:T(8,128)S(1)} %get-tuple-element.39), channel_id=1, source_target_pairs={{0,0},{4,1},{1,2},{5,3},{2,4},{6,5},{3,6},{7,7},{8,8},{12,9},{9,10... | collective-permute-start | bytes 1572872 | tf_op jit(solution)/shard_map/ppermute | solution.py:104
  236.2 15.5 %collective-permute-start.28 = (f32[2,512,128]{2,1,0:T(8,128)S(1)}, f32[2,512,128]{2,1,0:T(8,128)S(1)}, u32[]{:S(2)}, u32[]{:S(2)}) collective-permute-start(f32[2,512,128]{2,1,0:T(8,128)S(1)} %dynamic-slice_bitcast_fusion.13), channel_id=1, source_target_pairs={{0,4},{1,5},{2,6},{3,7},{4,0},{5,1},{6,2},{7,3},{8,12},{9,13},{10,... | collective-permute-start | bytes 1572872 | tf_op jit(solution)/shard_map/ppermute | solution.py:82
  248.2 23.8 %collective-permute-start.52 = (f32[512,256]{1,0:T(8,128)S(1)}, f32[512,256]{1,0:T(8,128)S(1)}, u32[]{:S(2)}, u32[]{:S(2)}) collective-permute-start(f32[512,256]{1,0:T(8,128)S(1)} %get-tuple-element.38), channel_id=1, source_target_pairs={{1,0},{5,1},{2,2},{6,3},{3,4},{7,5},{0,6},{4,7},{9,8},{13,9},{10,1... | collective-permute-start | bytes 1572872 | tf_op jit(solution)/shard_map/ppermute | solution.py:104
  251.9 15.9 %collective-permute-start.29 = (f32[1,512,128]{2,1,0:T(8,128)S(1)}, f32[1,512,128]{2,1,0:T(8,128)S(1)}, u32[]{:S(2)}, u32[]{:S(2)}) collective-permute-start(f32[1,512,128]{2,1,0:T(8,128)S(1)} %constant_dynamic-slice_fusion.12), channel_id=1, source_target_pairs={{0,2},{1,3},{2,0},{3,1},{4,6},{5,7},{6,4},{7,5},{8,10},{9,11},{10,... | collective-permute-start | bytes 786440 | tf_op jit(solution)/shard_map/ppermute | solution.py:82
  271.8 19.3 %collective-permute-start.60 = (f32[256,512]{1,0:T(8,128)S(1)}, f32[256,512]{1,0:T(8,128)S(1)}, u32[]{:S(2)}, u32[]{:S(2)}) collective-permute-start(f32[256,512]{1,0:T(8,128)S(1)} %dynamic-slice_bitcast_fusion), channel_id=1, source_target_pairs={{0,1},{1,0},{2,3},{3,2},{4,5},{5,4},{6,7},{7,6},{8,9},{9,8},{10,11... | collective-permute-start | bytes 1572872 | tf_op jit(solution)/shard_map/ppermute | solution.py:82
  286.6 47.0 %collective-permute-start.55 = (f32[4,512,256]{2,1,0:T(8,128)}, f32[4,512,256]{2,1,0:T(8,128)}, u32[]{:S(2)}, u32[]{:S(2)}) collective-permute-start(f32[4,512,256]{2,1,0:T(8,128)} %shard_map.66), channel_id=1, source_target_pairs={{0,1},{1,0},{2,3},{3,2},{4,5},{5,4},{6,7},{7,6},{8,9},{9,8},{10,11... | collective-permute-start | bytes 6291464 | tf_op jit(solution)/shard_map/ppermute | solution.py:82
  288.2 21.0 %collective-permute-start.41 = (f32[2,512,128]{2,1,0:T(8,128)S(1)}, f32[2,512,128]{2,1,0:T(8,128)S(1)}, u32[]{:S(2)}, u32[]{:S(2)}) collective-permute-start(f32[2,512,128]{2,1,0:T(8,128)S(1)} %dynamic-slice_bitcast_fusion.8), channel_id=1, source_target_pairs={{0,2},{1,3},{2,0},{3,1},{4,6},{5,7},{6,4},{7,5},{8,10},{9,11},{10,... | collective-permute-start | bytes 1572872 | tf_op jit(solution)/shard_map/ppermute | solution.py:82
  291.2 17.8 %collective-permute-start.61 = (f32[128,512]{1,0:T(8,128)S(1)}, f32[128,512]{1,0:T(8,128)S(1)}, u32[]{:S(2)}, u32[]{:S(2)}) collective-permute-start(f32[128,512]{1,0:T(8,128)S(1)} %dynamic-slice_bitcast_fusion.25), channel_id=1, source_target_pairs={{0,2},{1,3},{2,0},{3,1},{4,6},{5,7},{6,4},{7,5},{8,10},{9,11},{10,... | collective-permute-start | bytes 786440 | tf_op jit(solution)/shard_map/ppermute | solution.py:82
  333.6 15.3 %collective-permute-start.65 = (f32[64,512]{1,0:T(8,128)}, f32[64,512]{1,0:T(8,128)}, u32[]{:S(2)}, u32[]{:S(2)}) collective-permute-start(f32[64,512]{1,0:T(8,128)} %add.466), channel_id=1, source_target_pairs={{0,4},{1,5},{2,6},{3,7},{4,0},{5,1},{6,2},{7,3},{8,12},{9,13},{10,... | collective-permute-start | bytes 393224 | tf_op jit(solution)/shard_map/ppermute | solution.py:82
  343.8 15.5 %collective-permute-start.56 = (f32[2,512,128]{2,1,0:T(8,128)}, f32[2,512,128]{2,1,0:T(8,128)}, u32[]{:S(2)}, u32[]{:S(2)}) collective-permute-start(f32[2,512,128]{2,1,0:T(8,128)} %dynamic-slice_bitcast_fusion.2), channel_id=1, source_target_pairs={{0,2},{1,3},{2,0},{3,1},{4,6},{5,7},{6,4},{7,5},{8,10},{9,11},{10,... | collective-permute-start | bytes 1572872 | tf_op jit(solution)/shard_map/ppermute | solution.py:82
  345.0 16.6 %collective-permute-start.58 = (f32[2,512,128]{2,1,0:T(8,128)}, f32[2,512,128]{2,1,0:T(8,128)}, u32[]{:S(2)}, u32[]{:S(2)}) collective-permute-start(f32[2,512,128]{2,1,0:T(8,128)} %dynamic-slice_bitcast_fusion.1), channel_id=1, source_target_pairs={{0,4},{1,5},{2,6},{3,7},{4,0},{5,1},{6,2},{7,3},{8,12},{9,13},{10,... | collective-permute-start | bytes 1572872 | tf_op jit(solution)/shard_map/ppermute | solution.py:82
  378.3 24.0 %collective-permute-start.67 = (f32[256,512]{1,0:T(8,128)}, f32[256,512]{1,0:T(8,128)}, u32[]{:S(2)}, u32[]{:S(2)}) collective-permute-start(f32[256,512]{1,0:T(8,128)} %pad_maximum_fusion.6), channel_id=1, source_target_pairs={{0,1},{1,0},{2,3},{3,2},{4,5},{5,4},{6,7},{7,6},{8,9},{9,8},{10,11... | collective-permute-start | bytes 1572872 | tf_op jit(solution)/shard_map/ppermute | solution.py:82
  390.7 19.6 %collective-permute-start.75 = (f32[256,256]{1,0:T(8,128)S(1)}, f32[256,256]{1,0:T(8,128)S(1)}, u32[]{:S(2)}, u32[]{:S(2)}) collective-permute-start(f32[256,256]{1,0:T(8,128)S(1)} %pad_maximum_fusion.8), channel_id=1, source_target_pairs={{0,1},{1,0},{2,3},{3,2},{4,5},{5,4},{6,7},{7,6},{8,9},{9,8},{10,11... | collective-permute-start | bytes 786440 | tf_op jit(solution)/shard_map/ppermute | solution.py:82
  (47 other events, 431.6 us)
